TPU v7x, 32 devices: a whole 2x2x4 slice. The times are simulated.
32 devices in a mesh: section: 2 (over core), tensor: 8 (over z, y), dp: 2 (over x).
Axes of the slice: x: 2, y: 2, z: 4, core: 2. Of those that a mesh axis runs over, the one named last changes fastest.
Arguments:
- inputs: bfloat16 [8, 1024, 1024], P('dp', 'tensor'), may hold values from -6 to 6
- cotangent: bfloat16 [8, 1024, 1024], P('dp', 'tensor'), may hold values from -6 to 6
- norm_gain: bfloat16 [2, 1024], P('section'), may hold values from 0.5 to 1.5
- w_zx: bfloat16 [2, 1024, 2, 2048], P('section', None, None, 'tensor'), may hold values from -0.25 to 0.25
- w_bc: bfloat16 [2, 1024, 256], P('section'), may hold values from -0.1875 to 0.1875
- w_dt: bfloat16 [2, 1024, 32], P('section', None, 'tensor'), may hold values from -0.1875 to 0.1875
- dt_bias: float32 [2, 32], P('section', 'tensor'), may hold values from -6 to -2
- a_log: float32 [2, 32], P('section', 'tensor'), may hold values from 0 to 2.5
- d_skip: float32 [2, 32], P('section', 'tensor'), may hold values from 0.5 to 1.5
- conv_x_w: bfloat16 [2, 4, 2048], P('section', None, 'tensor'), may hold values from -3 to 3
- conv_x_b: bfloat16 [2, 2048], P('section', 'tensor'), may hold values from -3 to 3
- conv_bc_w: bfloat16 [2, 4, 256], P('section'), may hold values from -3 to 3
- conv_bc_b: bfloat16 [2, 256], P('section'), may hold values from -3 to 3
- gate_gain: bfloat16 [2, 2048], P('section', 'tensor'), may hold values from 0.5 to 1.5
- w_out: bfloat16 [2, 2048, 1024], P('section', 'tensor'), may hold values from -0.125 to 0.125
Outputs:
- section_out: bfloat16 [2, 8, 1024, 1024], P('section', 'dp', 'tensor')
- section_grad: float32 [2, 8, 1024, 1024], P('section', 'dp', 'tensor')
- grad_norm_gain: float32 [2, 1024], P('section')
- grad_w_zx: float32 [2, 1024, 2, 2048], P('section', None, None, 'tensor')
- grad_w_bc: float32 [2, 1024, 256], P('section')
- grad_w_dt: float32 [2, 1024, 32], P('section', None, 'tensor')
- grad_dt_bias: float32 [2, 32], P('section', 'tensor')
- grad_a_log: float32 [2, 32], P('section', 'tensor')
- grad_d_skip: float32 [2, 32], P('section', 'tensor')
- grad_conv_x_w: float32 [2, 4, 2048], P('section', None, 'tensor')
- grad_conv_x_b: float32 [2, 2048], P('section', 'tensor')
- grad_conv_bc_w: float32 [2, 4, 256], P('section')
- grad_conv_bc_b: float32 [2, 256], P('section')
- grad_gate_gain: float32 [2, 2048], P('section', 'tensor')
- grad_w_out: float32 [2, 2048, 1024], P('section', 'tensor')
All inputs are finite; a program needn't handle non-finite values.
Results may differ from a plain program's by a relative error of at most 0.019.
Values may be sent and summed in bfloat16 or wider, within the bound.
A program may use at most 256 MiB of HBM per device.

v0:
```python
import jax
import jax.numpy as jnp
from jax import lax
from jax.sharding import PartitionSpec as P

BLOCK = 256
INNER = 2048
SEQ_MB = 2


EPSILON = 1e-05
PRECISE = lax.Precision.HIGHEST


def shifted(block, axis, distance):
    devices = range(lax.axis_size(axis))
    route = [(i - distance, i) for i in devices if i - distance in devices]
    return lax.ppermute(block, axis, route)


def causal_conv(values, weight, biases):
    taps = weight.shape[0]
    length = values.shape[1]
    padded = jnp.pad(values, ((0, 0), (taps - 1, 0), (0, 0)))
    summed = biases
    for offset in range(taps):
        summed = summed + padded[:, offset : offset + length, :] * weight[offset]
    return jax.nn.silu(summed)


def state_scan(x_heads, deltas, decay_rate, b_matrix, c_matrix):
    seq_count, length, head_count, head_size = x_heads.shape
    state_size = b_matrix.shape[-1]
    block_count = length // BLOCK
    x_heads = x_heads.reshape(seq_count, block_count, BLOCK, head_count, head_size)
    deltas = deltas.reshape(seq_count, block_count, BLOCK, head_count)
    b_matrix = b_matrix.reshape(seq_count, block_count, BLOCK, state_size)
    c_matrix = c_matrix.reshape(seq_count, block_count, BLOCK, state_size)
    cumulative = jnp.cumsum(deltas * decay_rate, axis=2)
    differences = cumulative[:, :, :, None, :] - cumulative[:, :, None, :, :]
    causal = (jnp.arange(BLOCK)[:, None] >= jnp.arange(BLOCK)[None, :])[None, None, :, :, None]
    decays = jnp.where(causal, jnp.exp(jnp.minimum(differences, 0.0)), 0.0)
    affinity = jnp.einsum("nclk,ncmk->nclm", c_matrix, b_matrix, precision=PRECISE)
    weights = affinity[..., None] * decays * deltas[:, :, None, :, :]
    within = jnp.einsum("nclmh,ncmhp->nclhp", weights, x_heads, precision=PRECISE)
    closing = cumulative[:, :, -1, :]
    scaled = jnp.exp(closing[:, :, None, :] - cumulative) * deltas
    states = jnp.einsum("ncmh,ncmk,ncmhp->nchkp", scaled, b_matrix, x_heads, precision=PRECISE)

    def carry_step(running, pieces):
        block_state, fall_rate = pieces
        return (running * jnp.exp(fall_rate)[:, :, None, None] + block_state, running)

    initial = jnp.zeros((seq_count, head_count, state_size, head_size), x_heads.dtype)
    _, entering = lax.scan(
        carry_step, initial, (jnp.moveaxis(states, 1, 0), jnp.moveaxis(closing, 1, 0))
    )
    entering = jnp.moveaxis(entering, 0, 1)
    carried = (
        jnp.einsum("nclk,nchkp->nclhp", c_matrix, entering, precision=PRECISE)
        * jnp.exp(cumulative)[..., None]
    )
    return (within + carried).reshape(seq_count, length, head_count, head_size)


def mixer_part(
    z_and_x,
    b_and_c,
    dt_raw,
    conv_x_w,
    conv_x_b,
    conv_bc_w,
    conv_bc_b,
    dt_bias,
    a_log,
    d_skip,
    seq_count,
):
    row_count = z_and_x.shape[0]
    inner_size = z_and_x.shape[1] // 2
    head_count = dt_raw.shape[1]
    head_size = inner_size // head_count
    state_size = b_and_c.shape[1] // 2
    length = row_count // seq_count
    gate_in = z_and_x[:, :inner_size]
    x_conv = causal_conv(
        z_and_x[:, inner_size:].reshape(seq_count, length, inner_size), conv_x_w, conv_x_b
    )
    bc_conv = causal_conv(b_and_c.reshape(seq_count, length, 2 * state_size), conv_bc_w, conv_bc_b)
    deltas = jax.nn.softplus(dt_raw + dt_bias).reshape(seq_count, length, head_count)
    decay_rate = -jnp.exp(a_log)
    x_heads = x_conv.reshape(seq_count, length, head_count, head_size)
    scanned = state_scan(
        x_heads, deltas, decay_rate, bc_conv[..., :state_size], bc_conv[..., state_size:]
    )
    scanned = scanned + d_skip[:, None] * x_heads
    return scanned.reshape(row_count, inner_size) * jax.nn.silu(gate_in)


def contract_rows(left_side, right_side):
    return lax.dot_general(
        left_side, right_side, (((0,), (0,)), ((), ())), preferred_element_type=jnp.float32
    )


def contract_cols(left_side, right_side):
    return lax.dot_general(
        left_side, right_side, (((1,), (1,)), ((), ())), preferred_element_type=jnp.float32
    )


def take_block(buffer, slot_id):
    return lax.dynamic_index_in_dim(buffer, slot_id, 0, keepdims=False)


def put_block(buffer, slot_id, is_live, new_value):
    merged = jnp.where(is_live, new_value, take_block(buffer, slot_id))
    return lax.dynamic_update_index_in_dim(buffer, merged, slot_id, 0)


def masked(members, is_live):
    return tuple((jnp.where(is_live, member, 0.0) for member in members))


def body(
    inputs,
    cotangent,
    norm_gain,
    w_zx,
    w_bc,
    w_dt,
    dt_bias,
    a_log,
    d_skip,
    conv_x_w,
    conv_x_b,
    conv_bc_w,
    conv_bc_b,
    gate_gain,
    w_out,
):
    section_count = lax.axis_size("section")
    section_id = lax.axis_index("section")
    tensor_count = lax.axis_size("tensor")
    seq_dev, rows_own, model_width = inputs.shape
    length = rows_own * tensor_count
    micro_count = seq_dev // SEQ_MB
    row_count = SEQ_MB * length
    gain_float = norm_gain[0].astype(jnp.float32)
    inner_local = w_zx.shape[3]
    w_zx_flat = w_zx[0].reshape(model_width, 2 * inner_local)
    w_bc_local = w_bc[0]
    w_dt_local = w_dt[0]
    w_out_local = w_out[0]
    gate_own = gate_gain[0].astype(jnp.float32)
    small_params = (
        conv_x_w[0].astype(jnp.float32),
        conv_x_b[0].astype(jnp.float32),
        conv_bc_w[0].astype(jnp.float32),
        conv_bc_b[0].astype(jnp.float32),
        dt_bias[0],
        a_log[0],
        d_skip[0],
    )

    def local_mixer(
        z_and_x,
        b_and_c,
        dt_raw,
        conv_xw,
        conv_xb,
        conv_bcw,
        conv_bcb,
        bias_dt,
        log_rate,
        skip_weight,
    ):
        return mixer_part(
            z_and_x,
            b_and_c,
            dt_raw,
            conv_xw,
            conv_xb,
            conv_bcw,
            conv_bcb,
            bias_dt,
            log_rate,
            skip_weight,
            SEQ_MB,
        )

    def normalize(own_rows):
        hidden = own_rows.astype(jnp.float32)
        scale_in = lax.rsqrt(jnp.mean(hidden * hidden, axis=-1, keepdims=True) + EPSILON)
        normed_own = (hidden * scale_in * gain_float).astype(jnp.bfloat16)
        return (hidden, scale_in, normed_own)

    def projections(normed_full):
        normed = normed_full.reshape(row_count, model_width)
        z_and_x = jnp.dot(normed, w_zx_flat, preferred_element_type=jnp.float32)
        b_and_c = jnp.dot(normed, w_bc_local, preferred_element_type=jnp.float32)
        dt_raw = jnp.dot(normed, w_dt_local, preferred_element_type=jnp.float32)
        return (normed, z_and_x, b_and_c, dt_raw)

    def absorb(totals, sharded, shared):
        if totals is None:
            return (tuple(sharded), tuple(shared))
        return (
            tuple((total_now + member for total_now, member in zip(totals[0], sharded))),
            tuple((total_now + member for total_now, member in zip(totals[1], shared))),
        )

    input_blocks = inputs.reshape(micro_count, SEQ_MB, rows_own, model_width)
    seed_blocks = cotangent.reshape(micro_count, SEQ_MB, rows_own, model_width)
    received = jnp.zeros((SEQ_MB, rows_own, model_width), jnp.bfloat16)
    out_blocks = jnp.zeros((micro_count, SEQ_MB, rows_own, model_width), jnp.bfloat16)
    kept_rows = jnp.zeros((micro_count, SEQ_MB, rows_own, model_width), jnp.bfloat16)
    kept_scale = jnp.zeros((micro_count, row_count, 1), jnp.float32)
    kept_full = jnp.zeros((micro_count, SEQ_MB, length, model_width), jnp.bfloat16)
    for moment in range(micro_count + section_count - 1):
        batch_id = moment - section_id
        is_live = (batch_id >= 0) & (batch_id < micro_count)
        slot_id = jnp.clip(batch_id, 0, micro_count - 1)
        own_rows = jnp.where(section_id == 0, take_block(input_blocks, slot_id), received)
        forward_hidden, forward_scale_in, forward_normed_own = normalize(own_rows)
        forward_normed_full = lax.all_gather(forward_normed_own, "tensor", axis=1, tiled=True)
        forward_normed, forward_z_and_x, forward_b_and_c, forward_dt_raw = projections(
            forward_normed_full
        )
        forward_gated = local_mixer(forward_z_and_x, forward_b_and_c, forward_dt_raw, *small_params)
        squares = lax.psum(jnp.sum(forward_gated * forward_gated, axis=-1, keepdims=True), "tensor")
        forward_scale_gate = lax.rsqrt(squares / INNER + EPSILON)
        forward_mixed = (forward_gated * forward_scale_gate * gate_own).astype(jnp.bfloat16)
        partial_out = jnp.dot(
            forward_mixed, w_out_local, preferred_element_type=jnp.float32
        ).reshape(SEQ_MB, length, model_width)
        branch = lax.psum_scatter(partial_out, "tensor", scatter_dimension=1, tiled=True)
        result = forward_hidden + branch
        normed_full = forward_normed_full
        result_low = result.astype(jnp.bfloat16)
        received = shifted(result_low, "section", 1)
        out_blocks = put_block(out_blocks, slot_id, is_live, result_low)
        kept_rows = put_block(kept_rows, slot_id, is_live, own_rows)
        kept_scale = put_block(kept_scale, slot_id, is_live, forward_scale_gate)
        kept_full = put_block(kept_full, slot_id, is_live, normed_full)
    grad_blocks = jnp.zeros((micro_count, SEQ_MB, rows_own, model_width), jnp.float32)
    received_grad = jnp.zeros((SEQ_MB, rows_own, model_width), jnp.bfloat16)
    totals = None
    for moment in range(micro_count + section_count - 1):
        batch_id = micro_count - 1 - moment + (section_count - 1 - section_id)
        is_live = (batch_id >= 0) & (batch_id < micro_count)
        slot_id = jnp.clip(batch_id, 0, micro_count - 1)
        grad_rows = jnp.where(
            section_id == section_count - 1, take_block(seed_blocks, slot_id), received_grad
        )
        own_rows = take_block(kept_rows, slot_id)
        normed_full = take_block(kept_full, slot_id)
        backward_scale_gate = take_block(kept_scale, slot_id)
        backward_normed, backward_z_and_x, backward_b_and_c, backward_dt_raw = projections(
            normed_full
        )
        gated, pullback = jax.vjp(
            local_mixer, backward_z_and_x, backward_b_and_c, backward_dt_raw, *small_params
        )
        backward_mixed = (gated * backward_scale_gate * gate_own).astype(jnp.bfloat16)
        backward_grad_full = lax.all_gather(grad_rows, "tensor", axis=1, tiled=True).reshape(
            row_count, model_width
        )
        grad_mixed = contract_cols(backward_grad_full, w_out_local)
        grad_gate_gain = jnp.sum(grad_mixed * gated * backward_scale_gate, axis=0)
        gate_dot = lax.psum(
            jnp.sum(gated * gate_own * grad_mixed, axis=-1, keepdims=True), "tensor"
        )
        grad_gated = (
            backward_scale_gate * gate_own * grad_mixed
            - gated * backward_scale_gate**3 * gate_dot / INNER
        )
        pieces = pullback(grad_gated)
        backward_grad_zx = pieces[0].astype(jnp.bfloat16)
        backward_grad_bc = pieces[1].astype(jnp.bfloat16)
        backward_grad_dt = pieces[2].astype(jnp.bfloat16)
        grad_normed = (
            contract_cols(backward_grad_zx, w_zx_flat)
            + contract_cols(backward_grad_bc, w_bc_local)
            + contract_cols(backward_grad_dt, w_dt_local)
        )
        grad_norm_in = lax.psum_scatter(
            grad_normed.reshape(SEQ_MB, length, model_width).astype(jnp.bfloat16),
            "tensor",
            scatter_dimension=1,
            tiled=True,
        ).astype(jnp.float32)
        backward_hidden, backward_scale_in, unused_normed = normalize(own_rows)
        grad_gain_in = jnp.sum(grad_norm_in * backward_hidden * backward_scale_in, axis=(0, 1))
        norm_dot = jnp.sum(backward_hidden * gain_float * grad_norm_in, axis=-1, keepdims=True)
        grad_hidden = (
            grad_rows.astype(jnp.float32)
            + backward_scale_in * gain_float * grad_norm_in
            - backward_hidden * backward_scale_in**3 * norm_dot / model_width
        )
        backward_small_sharded = (
            pieces[3],
            pieces[4],
            pieces[7],
            pieces[8],
            pieces[9],
            grad_gate_gain,
        )
        backward_small_shared = (grad_gain_in, pieces[5], pieces[6])
        backward_saved = (
            backward_normed,
            backward_grad_zx,
            backward_grad_bc,
            backward_grad_dt,
            backward_mixed,
            backward_grad_full,
        )
        grad_hidden, small_sharded, small_shared, saved = (
            grad_hidden,
            backward_small_sharded,
            backward_small_shared,
            backward_saved,
        )
        received_grad = shifted(grad_hidden.astype(jnp.bfloat16), "section", -1)
        grad_blocks = put_block(grad_blocks, slot_id, is_live, grad_hidden)
        weight_normed, grad_zx, grad_bc, grad_dt, mixed, grad_full = saved
        heavy_sharded = (
            contract_rows(weight_normed, grad_zx),
            contract_rows(weight_normed, grad_dt),
            contract_rows(mixed, grad_full),
        )
        heavy_shared = (contract_rows(weight_normed, grad_bc),)
        finish_sharded = masked(heavy_sharded + small_sharded, is_live)
        finish_shared = masked(heavy_shared + small_shared, is_live)
        totals = absorb(totals, finish_sharded, finish_shared)
    sharded_totals, shared_totals = totals
    sharded_totals = (
        lax.psum(sharded_totals[0].astype(jnp.bfloat16), "dp").astype(jnp.float32),
        lax.psum(sharded_totals[1].astype(jnp.bfloat16), "dp").astype(jnp.float32),
        lax.psum(sharded_totals[2].astype(jnp.bfloat16), "dp").astype(jnp.float32),
        lax.psum(sharded_totals[3].astype(jnp.bfloat16), "dp").astype(jnp.float32),
        lax.psum(sharded_totals[4].astype(jnp.bfloat16), "dp").astype(jnp.float32),
        lax.psum(sharded_totals[5].astype(jnp.bfloat16), "dp").astype(jnp.float32),
        lax.psum(sharded_totals[6].astype(jnp.bfloat16), "dp").astype(jnp.float32),
        lax.psum(sharded_totals[7].astype(jnp.bfloat16), "dp").astype(jnp.float32),
        lax.psum(sharded_totals[8].astype(jnp.bfloat16), "dp").astype(jnp.float32),
    )
    shared_totals = lax.psum(
        (shared_totals[0], shared_totals[1], shared_totals[2], shared_totals[3]), ("tensor", "dp")
    )
    section_out = out_blocks.reshape(1, seq_dev, rows_own, model_width)
    section_grad = grad_blocks.reshape(1, seq_dev, rows_own, model_width)
    return (
        section_out,
        section_grad,
        shared_totals[1][None],
        sharded_totals[0].reshape(1, model_width, 2, inner_local),
        shared_totals[0][None],
        sharded_totals[1][None],
        sharded_totals[5][None],
        sharded_totals[6][None],
        sharded_totals[7][None],
        sharded_totals[3][None],
        sharded_totals[4][None],
        shared_totals[2][None],
        shared_totals[3][None],
        sharded_totals[8][None],
        sharded_totals[2][None],
    )


def solution(mesh):
    return jax.shard_map(
        body,
        mesh=mesh,
        in_specs=(
            P("dp", "tensor", None),
            P("dp", "tensor", None),
            P("section", None),
            P("section", None, None, "tensor"),
            P("section", None, None),
            P("section", None, "tensor"),
            P("section", "tensor"),
            P("section", "tensor"),
            P("section", "tensor"),
            P("section", None, "tensor"),
            P("section", "tensor"),
            P("section", None, None),
            P("section", None),
            P("section", "tensor"),
            P("section", "tensor", None),
        ),
        out_specs=(
            P("section", "dp", "tensor", None),
            P("section", "dp", "tensor", None),
            P("section", None),
            P("section", None, None, "tensor"),
            P("section", None, None),
            P("section", None, "tensor"),
            P("section", "tensor"),
            P("section", "tensor"),
            P("section", "tensor"),
            P("section", None, "tensor"),
            P("section", "tensor"),
            P("section", None, None),
            P("section", None),
            P("section", "tensor"),
            P("section", "tensor", None),
        ),
        check_vma=False,
    )
```

profile of v0, /device:TPU:0, one launch (start us, length us, event | category | flops | bytes accessed | tf_op | source)
XLA Modules:
  0.0 2380.1 jit_solution(15536104124070408312)
XLA Ops:
  12.2 75.5 %all-gather.8.cloned.1.call-done = bf16[2,1024,1024]{2,1,0:T(8,128)(2,1)} async-done(((bf16[2,128,1024]{2,1,0:T(8,128)(2,1)}), bf16[2,1024,1024]{2,1,0:T(8,128)(2,1)}) %all-gather.8.cloned.1.call-update) | async-done | bytes 4194320 | tf_op jit(solution)/shard_map/all_gather | solution.py:226
  91.2 9.6 reduce-window.60
  126.6 9.2 while.147
  143.9 9.7 bitcast_add_fusion.17
  166.6 18.9 psum.133
  192.1 146.4 %reduce-scatter.7.cloned.1.call-done = f32[2,128,1024]{2,1,0:T(8,128)} async-done(((f32[2,1024,1024]{2,1,0:T(8,128)}), f32[2,128,1024]{2,1,0:T(8,128)}) %reduce-scatter.7.cloned.1.call-update) | async-done | bytes 1048592 | tf_op jit(solution)/shard_map/reduce_scatter | solution.py:237
  347.5 73.7 %all-gather.10.cloned.1.call-done = bf16[2,1024,1024]{2,1,0:T(8,128)(2,1)} async-done(((bf16[2,128,1024]{2,1,0:T(8,128)(2,1)}), bf16[2,1024,1024]{2,1,0:T(8,128)(2,1)}) %all-gather.10.cloned.1.call-update) | async-done | bytes 4194320 | tf_op jit(solution)/shard_map/all_gather | solution.py:226
  433.2 10.1 reduce-window.64
  461.0 8.7 while.148
  478.0 11.1 bitcast_add_fusion.16
  504.3 18.9 psum.134
  531.8 144.4 %reduce-scatter.9.cloned.1.call-done = f32[2,128,1024]{2,1,0:T(8,128)} async-done(((f32[2,1024,1024]{2,1,0:T(8,128)}), f32[2,128,1024]{2,1,0:T(8,128)}) %reduce-scatter.9.cloned.1.call-update) | async-done | bytes 1048592 | tf_op jit(solution)/shard_map/reduce_scatter | solution.py:237
  699.6 57.7 %all-gather.12.cloned.1.call-done = bf16[2,1024,1024]{2,1,0:T(8,128)(2,1)} async-done(((bf16[2,128,1024]{2,1,0:T(8,128)(2,1)}), bf16[2,1024,1024]{2,1,0:T(8,128)(2,1)}) %all-gather.12.cloned.1.call-update) | async-done | bytes 4194320 | tf_op jit(solution)/shard_map/all_gather | solution.py:226
  757.3 6.3 bitcast_dynamic-update-slice_fusion.9
  763.6 8.6 constant_dynamic-slice_fusion.22
  787.3 9.6 reduce-window.70
  808.2 18.1 fusion.178
  846.1 11.3 fusion.179
  870.2 8.9 while.150
  888.7 11.1 bitcast_add_fusion.14
  912.6 9.6 reduce-window.66
  937.8 11.6 while.149
  956.4 9.7 bitcast_add_fusion.15
  979.4 18.9 psum.135
  1003.2 8.0 multiply_reduce_fusion.5
  1011.2 17.8 psum.136
  1053.9 18.8 while.151
  1078.0 6.8 fusion.297
  1087.0 17.4 fusion.442
  1104.4 9.1 bitcast_add_fusion.13
  1113.9 40.3 %reduce-window.74 = f32[2,4,4,2,128]{4,3,2,1,0:T(2,128)S(1)} reduce-window(f32[2,4,4,2,128]{4,3,2,1,0:T(2,128)S(1)} %reshape.1002, f32[]{:T(128)} %constant.418.clone.1), window={size=1x1x1x1x128 pad=0_0x0_0x0_0x0_0x0_127}, to_apply=%region_40.42 | reduce-window | flops 1040384 | bytes 65540 | tf_op jit(solution)/shard_map/reduce-window.8
  1198.7 9.6 reduce-window.76
  1208.6 74.4 %reduce-scatter.13.cloned.1.call-done = bf16[2,128,1024]{2,1,0:T(8,128)(2,1)} async-done(((bf16[2,1024,1024]{2,1,0:T(8,128)(2,1)}), bf16[2,128,1024]{2,1,0:T(8,128)(2,1)}) %reduce-scatter.13.cloned.1.call-update) | async-done | bytes 524304 | tf_op jit(solution)/shard_map/reduce_scatter | solution.py:287
  1307.9 18.6 while.152
  1336.1 11.2 bitcast_add_fusion.12
  1365.2 8.5 multiply_reduce_fusion.4
  1373.7 18.9 psum.137
  1392.6 6.8 fusion.159
  1419.1 19.0 while.153
  1443.7 7.8 fusion.302
  1453.7 17.4 fusion.440
  1471.1 9.0 bitcast_add_fusion.11
  1481.3 40.3 %reduce-window.80 = f32[2,4,4,2,128]{4,3,2,1,0:T(2,128)S(1)} reduce-window(f32[2,4,4,2,128]{4,3,2,1,0:T(2,128)S(1)} %reshape.1022, f32[]{:T(128)} %constant.418.clone.1), window={size=1x1x1x1x128 pad=0_0x0_0x0_0x0_0x0_127}, to_apply=%region_60.62 | reduce-window | flops 1040384 | bytes 65540 | tf_op jit(solution)/shard_map/reduce-window.12
  1549.5 6.9 multiply_reduce_fusion.24
  1588.0 65.3 %reduce-scatter.15.cloned.1.call-done = bf16[2,128,1024]{2,1,0:T(8,128)(2,1)} async-done(((bf16[2,1024,1024]{2,1,0:T(8,128)(2,1)}), bf16[2,128,1024]{2,1,0:T(8,128)(2,1)}) %reduce-scatter.15.cloned.1.call-update) | async-done | bytes 524304 | tf_op jit(solution)/shard_map/reduce_scatter | solution.py:287
  1660.9 9.6 reduce-window.84
  1682.5 18.7 while.154
  1709.0 11.2 bitcast_add_fusion.10
  1730.3 7.3 fusion.445
  1737.6 9.4 all-gather.16.cloned.1.call-done
  1747.0 8.5 multiply_reduce_fusion.3
  1755.6 18.9 psum.138
  1774.5 7.5 fusion.157
  1796.7 18.7 while.155
  1823.1 9.0 bitcast_add_fusion.9
  1832.2 17.4 fusion.438
  1854.4 7.8 fusion.307
  1876.1 40.3 %reduce-window.86 = f32[2,4,4,2,128]{4,3,2,1,0:T(2,128)S(1)} reduce-window(f32[2,4,4,2,128]{4,3,2,1,0:T(2,128)S(1)} %reshape.1042, f32[]{:T(128)} %constant.418.clone.1), window={size=1x1x1x1x128 pad=0_0x0_0x0_0x0_0x0_127}, to_apply=%region_80.82 | reduce-window | flops 1040384 | bytes 65540 | tf_op jit(solution)/shard_map/reduce-window.16
  1965.5 6.7 add_convert_fusion
  1999.0 8.4 all-reduce.76
  2022.3 78.4 %reduce-scatter.17.cloned.1.call-done = bf16[2,128,1024]{2,1,0:T(8,128)(2,1)} async-done(((bf16[2,1024,1024]{2,1,0:T(8,128)(2,1)}), bf16[2,128,1024]{2,1,0:T(8,128)(2,1)}) %reduce-scatter.17.cloned.1.call-update) | async-done | bytes 524304 | tf_op jit(solution)/shard_map/reduce_scatter | solution.py:287
  2102.4 45.0 %all-reduce.75 = (f32[1,1024]{1,0:T(1,128)}, f32[1,4,256]{2,1,0:T(4,128)}, f32[1,256]{1,0:T(1,128)}) all-reduce(f32[1,1024]{1,0:T(1,128)S(1)} %bitcast.1302, f32[1,4,256]{2,1,0:T(4,128)S(1)} %add_bitcast_fusion.3, f32[1,256]{1,0:T(1,128)S(1)} %bitcast.1333), channel_id=1, replica_groups=mesh['section'=2,'tensor'=8,'dp'=2] {'tensor','dp'}, use_global_device_ids=true, to_apply=%region_87.89 | all-reduce | flops 2304 | bytes 18432 | tf_op jit(solution)/shard_map/psum | solution.py:348
  2150.8 103.6 %reduce-scatter.11.cloned.1.call-done = f32[2,128,1024]{2,1,0:T(8,128)} async-done(((f32[2,1024,1024]{2,1,0:T(8,128)}), f32[2,128,1024]{2,1,0:T(8,128)}) %reduce-scatter.11.cloned.1.call-update) | async-done | bytes 1048592 | tf_op jit(solution)/shard_map/reduce_scatter | solution.py:237
  2256.7 114.5 %all-reduce.81.cloned.1.call-done = f32[1,1024,256]{2,1,0:T(8,128)} async-done(((f32[1,1024,256]{2,1,0:T(8,128)}), f32[1,1024,256]{2,1,0:T(8,128)}) %all-reduce.81.cloned.1.call-update) | async-done | bytes 1048592 | tf_op jit(solution)/shard_map/psum | solution.py:348
  (1246 shorter events, 801.6 us)
Async XLA Ops:
  7.2 180.3 %copy-start = (bf16[1,256,1024]{2,1,0:T(8,128)(2,1)S(1)}, bf16[1,256,1024]{2,1,0:T(8,128)(2,1)}, u32[]{:S(2)}) copy-start(bf16[1,256,1024]{2,1,0:T(8,128)(2,1)} %param.48) | copy-start | bytes 1572868
  7.2 80.5 %all-gather.8.cloned.1.call-start = ((), (), s32[]{:S(2)}) async-start(), calls=%async_computation.6 | async-start | bytes 4718592 | tf_op jit(solution)/shard_map/all_gather | solution.py:226
  7.3 80.3 %copy-start.150 = (bf16[1,1024,4]{1,2,0:T(4,128)(2,1)S(1)}, bf16[1,1024,4]{1,2,0:T(4,128)(2,1)}, u32[]{:S(2)}) copy-start(bf16[1,1024,4]{1,2,0:T(4,128)(2,1)} %param.39) | copy-start | bytes 24580
  7.3 80.3 %copy-start.181 = (f32[1,4]{1,0:T(1,128)S(1)}, f32[1,4]{1,0:T(1,128)}, u32[]{:S(2)}) copy-start(f32[1,4]{1,0:T(1,128)} %param.40) | copy-start | bytes 52
  9.4 673.5 %copy-start.163 = (f32[1,1024]{1,0:T(1,128)}, f32[1,1024]{1,0:T(1,128)S(1)}, u32[]{:S(2)}) copy-start(f32[1,1024]{1,0:T(1,128)S(1)} %convert_element_type.295) | copy-start | bytes 12292
  11.4 327.1 %reduce-scatter.7.cloned.1.call-start = ((), (), s32[]{:S(2)}) async-start(), calls=%async_computation.7 | async-start | bytes 9437184 | tf_op jit(solution)/shard_map/reduce_scatter | solution.py:237
  11.8 90.0 %copy-start.141 = (bf16[128,8,2,256]{3,1,2,0:T(8,128)(2,1)}, bf16[128,8,2,256]{3,1,2,0:T(8,128)(2,1)S(1)}, u32[]{:S(2)}) copy-start(bf16[128,8,2,256]{3,1,2,0:T(8,128)(2,1)S(1)} %copy.1339) | copy-start | bytes 3145732
  11.8 432.3 %copy-start.234 = (f32[1,256]{1,0:T(1,128)}, f32[1,256]{1,0:T(1,128)S(1)}, u32[]{:S(2)}) copy-start(f32[1,256]{1,0:T(1,128)S(1)} %convert_element_type.294) | copy-start | bytes 3076
  11.8 418.8 %copy-start.236 = (f32[1,256]{1,0:T(1,128)}, f32[1,256]{1,0:T(1,128)S(1)}, u32[]{:S(2)}) copy-start(f32[1,256]{1,0:T(1,128)S(1)} %convert_element_type.296) | copy-start | bytes 3076
  12.0 1168.9 %copy-start.172 = (f32[256]{0:T(256)}, f32[256]{0:T(256)S(1)}, u32[]{:S(2)}) copy-start(f32[256]{0:T(256)S(1)} %mul.1905) | copy-start | bytes 3076
  12.0 511.3 %copy-start.189 = (f32[1,256]{1,0:T(1,128)}, f32[1,256]{1,0:T(1,128)S(1)}, u32[]{:S(2)}) copy-start(f32[1,256]{1,0:T(1,128)S(1)} %mul.2267) | copy-start | bytes 3076
  12.0 875.4 %copy-start.184 = (pred[256,256]{1,0:T(8,128)(4,1)}, pred[256,256]{1,0:T(8,128)(4,1)S(1)}, u32[]{:S(2)}) copy-start(pred[256,256]{1,0:T(8,128)(4,1)S(1)} %iota_compare_fusion) | copy-start | bytes 196612
  12.1 774.5 %copy-start.230 = (f32[4]{0:T(128)}, f32[4]{0:T(128)S(1)}, u32[]{:S(2)}) copy-start(f32[4]{0:T(128)S(1)} %bitcast_negate_fusion) | copy-start | bytes 52
  12.1 833.6 %copy-start.193 = (f32[1,1,256]{2,1,0:T(1,128)}, f32[1,1,256]{2,1,0:T(1,128)S(1)}, u32[]{:S(2)}) copy-start(f32[1,1,256]{2,1,0:T(1,128)S(1)} %get-tuple-element.1677) | copy-start | bytes 3076
  12.1 833.6 %copy-start.197 = (f32[1,1,256]{2,1,0:T(1,128)}, f32[1,1,256]{2,1,0:T(1,128)S(1)}, u32[]{:S(2)}) copy-start(f32[1,1,256]{2,1,0:T(1,128)S(1)} %get-tuple-element.1678) | copy-start | bytes 3076
  12.1 833.6 %copy-start.201 = (f32[1,1,256]{2,1,0:T(1,128)}, f32[1,1,256]{2,1,0:T(1,128)S(1)}, u32[]{:S(2)}) copy-start(f32[1,1,256]{2,1,0:T(1,128)S(1)} %get-tuple-element.1679) | copy-start | bytes 3076
  12.1 833.6 %copy-start.205 = (f32[1,1,256]{2,1,0:T(1,128)}, f32[1,1,256]{2,1,0:T(1,128)S(1)}, u32[]{:S(2)}) copy-start(f32[1,1,256]{2,1,0:T(1,128)S(1)} %get-tuple-element.1680) | copy-start | bytes 3076
  12.2 796.0 %copy-start.209 = (f32[1,1,256]{2,1,0:T(1,128)}, f32[1,1,256]{2,1,0:T(1,128)S(1)}, u32[]{:S(2)}) copy-start(f32[1,1,256]{2,1,0:T(1,128)S(1)} %get-tuple-element.1681) | copy-start | bytes 3076
  12.2 796.0 %copy-start.213 = (f32[1,1,256]{2,1,0:T(1,128)}, f32[1,1,256]{2,1,0:T(1,128)S(1)}, u32[]{:S(2)}) copy-start(f32[1,1,256]{2,1,0:T(1,128)S(1)} %get-tuple-element.1682) | copy-start | bytes 3076
  12.2 795.9 %copy-start.217 = (f32[1,1,256]{2,1,0:T(1,128)}, f32[1,1,256]{2,1,0:T(1,128)S(1)}, u32[]{:S(2)}) copy-start(f32[1,1,256]{2,1,0:T(1,128)S(1)} %get-tuple-element.1683) | copy-start | bytes 3076
  12.2 795.9 %copy-start.221 = (f32[1,1,256]{2,1,0:T(1,128)}, f32[1,1,256]{2,1,0:T(1,128)S(1)}, u32[]{:S(2)}) copy-start(f32[1,1,256]{2,1,0:T(1,128)S(1)} %get-tuple-element.1684) | copy-start | bytes 3076
  192.1 147.5 %copy-start.61 = (bf16[4,128,1024]{2,1,0:T(8,128)(2,1)S(1)}, bf16[4,128,1024]{2,1,0:T(8,128)(2,1)}, u32[]{:S(2)}) copy-start(bf16[4,128,1024]{2,1,0:T(8,128)(2,1)} %param.34) | copy-start | bytes 3145732
  192.1 229.1 %all-gather.10.cloned.1.call-start = ((), (), s32[]{:S(2)}) async-start(), calls=%async_computation.8 | async-start | bytes 4718592 | tf_op jit(solution)/shard_map/all_gather | solution.py:226
  341.9 3.4 collective-permute-start
  347.4 328.8 %reduce-scatter.9.cloned.1.call-start = ((), (), s32[]{:S(2)}) async-start(), calls=%async_computation.9 | async-start | bytes 9437184 | tf_op jit(solution)/shard_map/reduce_scatter | solution.py:237
  433.1 23.3 copy-start.67
  529.8 146.4 %copy-start.95 = (bf16[2,128,1024]{2,1,0:T(8,128)(2,1)S(1)}, bf16[2,128,1024]{2,1,0:T(8,128)(2,1)}, u32[]{:S(2)}) copy-start(bf16[2,128,1024]{2,1,0:T(8,128)(2,1)} %copy-done.94) | copy-start | bytes 1572868
  529.8 227.5 %all-gather.12.cloned.1.call-start = ((), (), s32[]{:S(2)}) async-start(), calls=%async_computation.10 | async-start | bytes 4718592 | tf_op jit(solution)/shard_map/all_gather | solution.py:226
  531.8 150.6 %copy-start.62 = (bf16[4,128,1024]{2,1,0:T(8,128)(2,1)S(1)}, bf16[4,128,1024]{2,1,0:T(8,128)(2,1)}, u32[]{:S(2)}) copy-start(bf16[4,128,1024]{2,1,0:T(8,128)(2,1)} %param.34) | copy-start | bytes 3145732
  678.8 3.5 collective-permute-start.1
  684.5 318.7 %all-gather.18.cloned.1.call-start = ((), (), s32[]{:S(2)}) async-start(), calls=%async_computation.18 | async-start | bytes 4718592 | tf_op jit(solution)/shard_map/all_gather | solution.py:266
  686.5 596.5 %reduce-scatter.13.cloned.1.call-start = ((), (), s32[]{:S(2)}) async-start(), calls=%async_computation.12 | async-start | bytes 4718592 | tf_op jit(solution)/shard_map/reduce_scatter | solution.py:287
  699.6 57.7 %copy-start.158 = (f32[2,2048,1]{1,2,0:T(1,128)}, f32[2,2048,1]{1,2,0:T(1,128)S(1)}, u32[]{:S(2)}) copy-start(f32[2,2048,1]{1,2,0:T(1,128)S(1)} %constant_dynamic-update-slice_fusion.7) | copy-start | bytes 49156
  797.9 89.6 %copy-start.152 = (f32[2,4,256,4]{2,3,1,0:T(4,128)}, f32[2,4,256,4]{2,3,1,0:T(4,128)S(1)}, u32[]{:S(2)}) copy-start(f32[2,4,256,4]{2,3,1,0:T(4,128)S(1)} %get-tuple-element.1656) | copy-start | bytes 98308
  829.2 34.7 %copy-start.24 = (f32[2,1024,128]{2,1,0:T(8,128)}, f32[2,1024,128]{2,1,0:T(8,128)S(1)}, u32[]{:S(2)}) copy-start(f32[2,1024,128]{2,1,0:T(8,128)S(1)} %get-tuple-element.1638) | copy-start | bytes 3145732
  975.1 23.2 copy-start.159
  975.1 23.9 %copy-start.182 = (f32[1,4]{1,0:T(1,128)S(1)}, f32[1,4]{1,0:T(1,128)}, u32[]{:S(2)}) copy-start(f32[1,4]{1,0:T(1,128)} %param.40) | copy-start | bytes 52
  999.0 30.0 %copy-start.177 = (f32[1,2048,1]{1,2,0:T(1,128)}, f32[1,2048,1]{1,2,0:T(1,128)S(1)}, u32[]{:S(2)}) copy-start(f32[1,2048,1]{1,2,0:T(1,128)S(1)} %get-tuple-element.1666) | copy-start | bytes 24580
  1053.9 18.8 copy-start.26
  1196.5 86.5 %copy-start.108 = (bf16[1,2,128,1024]{3,2,1,0:T(8,128)(2,1)S(1)}, bf16[1,2,128,1024]{3,2,1,0:T(8,128)(2,1)}, u32[]{:S(2)}) copy-start(bf16[1,2,128,1024]{3,2,1,0:T(8,128)(2,1)} %dynamic-slice_select_fusion) | copy-start | bytes 1572868
  1196.5 86.5 %copy-start.164 = (f32[1,1024]{1,0:T(1,128)S(1)}, f32[1,1024]{1,0:T(1,128)}, u32[]{:S(2)}) copy-start(f32[1,1024]{1,0:T(1,128)} %copy-done.163) | copy-start | bytes 12292
  1196.5 168.6 %all-gather.14.cloned.1.call-start = ((), (), s32[]{:S(2)}) async-start(), calls=%async_computation.13 | async-start | bytes 4718592 | tf_op jit(solution)/shard_map/all_gather | solution.py:266
  1198.6 93.2 %copy-start.238 = (f32[2,128]{1,0:T(2,128)}, f32[2,128]{1,0:T(2,128)S(1)}, u32[]{:S(2)}) copy-start(f32[2,128]{1,0:T(2,128)S(1)} %get-tuple-element.1690) | copy-start | bytes 3076
  1286.0 4.0 collective-permute-start.2
  1291.9 361.4 %reduce-scatter.15.cloned.1.call-start = ((), (), s32[]{:S(2)}) async-start(), calls=%async_computation.14 | async-start | bytes 4718592 | tf_op jit(solution)/shard_map/reduce_scatter | solution.py:287
  1292.9 41.9 %copy-start.154 = (f32[2,4,256,4]{2,3,1,0:T(4,128)}, f32[2,4,256,4]{2,3,1,0:T(4,128)S(1)}, u32[]{:S(2)}) copy-start(f32[2,4,256,4]{2,3,1,0:T(4,128)S(1)} %get-tuple-element.1654) | copy-start | bytes 98308
  1471.1 50.9 %copy-start.31 = (f32[2,1024,128]{2,1,0:T(8,128)S(1)}, f32[2,1024,128]{2,1,0:T(8,128)}, u32[]{:S(2)}) copy-start(f32[2,1024,128]{2,1,0:T(8,128)} %copy-done.29) | copy-start | bytes 3145732
  1567.8 179.2 %all-gather.16.cloned.1.call-start = ((), (), s32[]{:S(2)}) async-start(), calls=%async_computation.15 | async-start | bytes 4718592 | tf_op jit(solution)/shard_map/all_gather | solution.py:266
  1568.4 84.8 %copy-start.240 = (f32[2,128]{1,0:T(2,128)}, f32[2,128]{1,0:T(2,128)S(1)}, u32[]{:S(2)}) copy-start(f32[2,128]{1,0:T(2,128)S(1)} %get-tuple-element.1688) | copy-start | bytes 3076
  1584.2 69.1 %copy-start.109 = (bf16[2,128,1024]{2,1,0:T(8,128)(2,1)S(1)}, bf16[2,128,1024]{2,1,0:T(8,128)(2,1)}, u32[]{:S(2)}) copy-start(bf16[2,128,1024]{2,1,0:T(8,128)(2,1)} %bitcast_select_fusion.4) | copy-start | bytes 1572868
  1656.4 14.6 collective-permute-start.3
  1672.9 344.8 %all-reduce.83.cloned.1.call-start = ((), (), s32[]{:S(2)}) async-start(), calls=%async_computation.19 | async-start | bytes 3145728 | tf_op jit(solution)/shard_map/psum | solution.py:338
  1747.0 27.5 %copy-start.225 = (f32[2048]{0:T(1024)S(1)}, f32[2048]{0:T(1024)}, u32[]{:S(2)}) copy-start(f32[2048]{0:T(1024)} %multiply_multiply_fusion.3) | copy-start | bytes 24580
  1747.0 27.5 %copy-start.226 = (f32[2048,1]{0,1:T(1,128)S(1)}, f32[2048,1]{0,1:T(1,128)}, u32[]{:S(2)}) copy-start(f32[2048,1]{0,1:T(1,128)} %add_rsqrt_fusion) | copy-start | bytes 24580
  1832.2 17.4 copy-start.64
  1869.4 47.4 %copy-start.28 = (f32[2,1024,128]{2,1,0:T(8,128)S(1)}, f32[2,1024,128]{2,1,0:T(8,128)}, u32[]{:S(2)}) copy-start(f32[2,1024,128]{2,1,0:T(8,128)} %get-tuple-element.1618) | copy-start | bytes 3145732
  1959.2 141.4 %reduce-scatter.17.cloned.1.call-start = ((), (), s32[]{:S(2)}) async-start(), calls=%async_computation.16 | async-start | bytes 4718592 | tf_op jit(solution)/shard_map/reduce_scatter | solution.py:287
  1972.2 282.2 %reduce-scatter.11.cloned.1.call-start = ((), (), s32[]{:S(2)}) async-start(), calls=%async_computation.11 | async-start | bytes 9437184 | tf_op jit(solution)/shard_map/reduce_scatter | solution.py:237
  1978.0 393.2 %all-reduce.81.cloned.1.call-start = ((), (), s32[]{:S(2)}) async-start(), calls=%async_computation.17 | async-start | bytes 2097152 | tf_op jit(solution)/shard_map/psum | solution.py:348
  2017.8 82.8 %copy-start.139 = (bf16[2,128,1024]{2,1,0:T(8,128)(2,1)S(1)}, bf16[2,128,1024]{2,1,0:T(8,128)(2,1)}, u32[]{:S(2)}) copy-start(bf16[2,128,1024]{2,1,0:T(8,128)(2,1)} %reduce-scatter.13.cloned.1.call-done) | copy-start | bytes 1572868
  2017.8 82.8 %copy-start.239 = (f32[2,128]{1,0:T(2,128)S(1)}, f32[2,128]{1,0:T(2,128)}, u32[]{:S(2)}) copy-start(f32[2,128]{1,0:T(2,128)} %copy-done.238) | copy-start | bytes 3076
  2017.8 82.8 %copy-start.241 = (f32[2,128]{1,0:T(2,128)S(1)}, f32[2,128]{1,0:T(2,128)}, u32[]{:S(2)}) copy-start(f32[2,128]{1,0:T(2,128)} %copy-done.240) | copy-start | bytes 3076
  2021.2 126.3 %copy-start.134 = (bf16[2,128,1024]{2,1,0:T(8,128)(2,1)S(1)}, bf16[2,128,1024]{2,1,0:T(8,128)(2,1)}, u32[]{:S(2)}) copy-start(bf16[2,128,1024]{2,1,0:T(8,128)(2,1)} %bitcast_select_fusion.3) | copy-start | bytes 1572868
  2147.4 107.0 %copy-start.93 = (bf16[2,128,1024]{2,1,0:T(8,128)(2,1)S(1)}, bf16[2,128,1024]{2,1,0:T(8,128)(2,1)}, u32[]{:S(2)}) copy-start(bf16[2,128,1024]{2,1,0:T(8,128)(2,1)} %copy-done.92) | copy-start | bytes 1572868
  (244 other events, 925.6 us)
Sparse Core Ops, SparseCore 0:
  11.6 76.0 all-gather.7
  192.2 146.2 reduce-scatter.6
  347.5 73.6 all-gather.9
  529.9 146.2 reduce-scatter.8
  684.6 72.6 all-gather.11
  759.4 71.6 all-gather.17
  1196.7 86.2 reduce-scatter.12
  1292.0 73.1 all-gather.13
  1567.9 85.2 reduce-scatter.14
  1673.1 73.9 all-gather.15
  1959.4 49.2 all-reduce.82
  2012.5 88.0 reduce-scatter.16
  2104.3 150.0 reduce-scatter.10
  2260.4 110.7 all-reduce.80
where the time goes:
time: 2400 us; the launch traced here: 2380 us
  waiting for transfers between devices  951 us (40%)
  matrix products  456 us (19%)
  other arithmetic  433 us (18%)
  local copies, waits for them, and re-layouts  346 us (14%)
  blocking collectives  166 us (7%)
    reduce_scatter x3, waiting for transfers between devices, body(): lax.psum_scatter(partial_out, 'tensor', scatter_dimension=1, tiled=True)  394 us
    reduce_scatter x3, waiting for transfers between devices, body(): lax.psum_scatter(grad_normed.reshape(SEQ_MB, length, model_width).astype(...  218 us
    all_gather x3, waiting for transfers between devices, body(): lax.all_gather(forward_normed_own, 'tensor', axis=1, tiled=True)  207 us
    another operation x35, other arithmetic  187 us
    dot_general x12, matrix products, state_scan(): jnp.einsum('nclmh,ncmhp->nclhp', weights, x_heads, precision=PRECISE)  143 us
    psum x1, waiting for transfers between devices, body(): lax.psum((shared_totals[0], shared_totals[1], shared_totals[2], shared_to...  115 us
    reshape x15, local copies, waits for them, and re-layouts, state_scan(): return (within + carried).reshape(seq_count, length, head_count, head_size)  68.5 us
    dot_general x12, matrix products, contract_cols(): lax.dot_general(left_side, right_side, (((1,), (1,)), ((), ())), preferre...  62.9 us
  transfers between devices with their start and end apart: 18, of which 15 were waited for; matrix products, arithmetic and copies ran while one was open for 19% of the time, Pallas kernels for 0%

commit v1 on v0

v1 whole, which is shorter than its diff:
```python
import functools

import jax
import jax.numpy as jnp
from jax import lax
from jax.experimental import pallas as pl
from jax.experimental.pallas import tpu as pltpu
from jax.sharding import PartitionSpec as P

BLOCK = 256
HEAD = 64
DTW = 128
EPSILON = 1e-05
F32 = jnp.float32
BF16 = jnp.bfloat16
VMEM_BYTES = 48 * 1024 * 1024

DIMS = {"nn": ((1,), (0,)), "nt": ((1,), (1,)), "tn": ((0,), (0,))}


def plain_dot(a, b, mode, exact):
    if exact:
        return lax.dot_general(
            a, b, (DIMS[mode], ((), ())), precision=lax.Precision.HIGHEST, preferred_element_type=F32
        )
    return lax.dot_general(
        a.astype(BF16), b.astype(BF16), (DIMS[mode], ((), ())), preferred_element_type=F32
    )


def make_dot(mode, exact):
    @jax.custom_vjp
    def dot(a, b):
        return plain_dot(a, b, mode, exact)

    def keep(a, b):
        return plain_dot(a, b, mode, exact), (a, b)

    def back(kept, g):
        a, b = kept
        if mode == "nn":
            return plain_dot(g, b, "nt", exact), plain_dot(a, g, "tn", exact)
        if mode == "nt":
            return plain_dot(g, b, "nn", exact), plain_dot(g, a, "tn", exact)
        return plain_dot(b, g, "nt", exact), plain_dot(a, g, "nn", exact)

    dot.defvjp(keep, back)
    return dot


dot_nn = make_dot("nn", False)
dot_nt = make_dot("nt", False)
dot_tn = make_dot("tn", False)
exact_nn = make_dot("nn", True)


@jax.custom_vjp
def softplus(v):
    return jnp.maximum(v, 0.0) + jnp.log1p(jnp.exp(-jnp.abs(v)))


softplus.defvjp(lambda v: (softplus(v), v), lambda v, g: (g * lax.logistic(v),))


@functools.partial(jax.custom_vjp, nondiff_argnums=(2,))
def delayed(halo, values, distance):
    joined = jnp.concatenate([halo, values], axis=0)
    if distance:
        joined = pltpu.roll(joined, distance, 0)
    return joined[8:]


def delayed_keep(halo, values, distance):
    return delayed(halo, values, distance), None


def delayed_back(distance, kept, g):
    joined = jnp.concatenate([jnp.zeros((8, g.shape[1]), g.dtype), g], axis=0)
    if distance:
        joined = pltpu.roll(joined, joined.shape[0] - distance, 0)
    return joined[:8], joined[8:]


delayed.defvjp(delayed_keep, delayed_back)


def conv_silu(halo, values, taps, bias):
    count = len(taps)
    summed = bias + values * taps[count - 1]
    for k in range(count - 1):
        summed = summed + delayed(halo, values, count - 1 - k) * taps[k]
    return summed * lax.logistic(summed)


def block_mixer(z, x, b, c, dt, hx, hb, hc, state, xt, bt, ct, xb, bb, cb, dt_bias, a_log, skip):
    rows, inner = x.shape
    heads = inner // HEAD
    xc = conv_silu(hx, x, xt, xb)
    bm = conv_silu(hb, b, bt, bb)
    cm = conv_silu(hc, c, ct, cb)
    delta = softplus(dt + dt_bias)
    falls = delta * (-jnp.exp(a_log))
    row_id = lax.broadcasted_iota(jnp.int32, (rows, rows), 0)
    col_id = lax.broadcasted_iota(jnp.int32, (rows, rows), 1)
    causal = row_id >= col_id
    cum = exact_nn(jnp.where(causal, 1.0, 0.0).astype(F32), falls)
    closing = jnp.sum(falls, axis=0, keepdims=True)
    spread_row = lax.broadcasted_iota(jnp.int32, (DTW, inner), 0)
    spread_col = lax.broadcasted_iota(jnp.int32, (DTW, inner), 1)
    spread = jnp.where(
        (spread_col >= spread_row * HEAD) & (spread_col < (spread_row + 1) * HEAD), 1.0, 0.0
    ).astype(F32)
    xd = xc * exact_nn(delta, spread)
    cum_t = jnp.transpose(cum)
    affinity = dot_nt(cm, bm)
    lane = lax.broadcasted_iota(jnp.int32, (rows, DTW), 1)
    sub = lax.broadcasted_iota(jnp.int32, (DTW, rows), 0)
    chan = lax.broadcasted_iota(jnp.int32, (rows, inner), 1)
    y = dot_nn(cm, state) * exact_nn(jnp.exp(cum), spread) + skip * xc
    for h in range(heads):
        col = jnp.sum(jnp.where(lane == h, cum, 0.0), axis=1, keepdims=True)
        row = jnp.sum(jnp.where(sub == h, cum_t, 0.0), axis=0, keepdims=True)
        decay = jnp.exp(jnp.where(causal, col - row, -1e30))
        own = (chan >= h * HEAD) & (chan < (h + 1) * HEAD)
        y = y + dot_nn(affinity * decay, jnp.where(own, xd, 0.0))
    leaving = jnp.broadcast_to(jnp.exp(closing) * 0.125, (8, DTW))
    kept = jnp.sum(exact_nn(leaving, spread), axis=0, keepdims=True)
    scaled = xd * exact_nn(jnp.exp(closing - cum), spread)
    state_out = state * kept + dot_tn(bm, scaled)
    return y * (z * lax.logistic(z)), state_out


def block_args(proj, halo, live, par_x, par_bc, par_dt, inner):
    z = proj[:, :inner]
    x = proj[:, inner : 2 * inner]
    at = 2 * inner
    b = proj[:, at : at + 128]
    c = proj[:, at + 128 : at + 256]
    dt = proj[:, at + 256 : at + 256 + DTW]
    hx = halo[:, inner : 2 * inner] * live
    hb = halo[:, at : at + 128] * live
    hc = halo[:, at + 128 : at + 256] * live
    xt = [par_x[k : k + 1, :] for k in range(4)]
    bt = [par_bc[k : k + 1, :128] for k in range(4)]
    ct = [par_bc[k : k + 1, 128:] for k in range(4)]
    tail = (
        xt, bt, ct,
        par_x[4:5, :], par_bc[4:5, :128], par_bc[4:5, 128:],
        par_dt[0:1, :], par_dt[1:2, :], par_x[5:6, :],
    )
    return (z, x, b, c, dt, hx, hb, hc), tail


def forward_kernel(proj, halo, par_x, par_bc, par_dt, g_out, state_out, state):
    inner = par_x.shape[1]
    step = pl.program_id(0)

    @pl.when(step == 0)
    def _():
        state[...] = jnp.zeros_like(state)

    live = jnp.where(step > 0, 1.0, 0.0).astype(F32)
    head, tail = block_args(proj, halo, live, par_x, par_bc, par_dt, inner)
    entering = state[...]
    state_out[0] = entering
    g, leaving = block_mixer(*head, entering, *tail)
    g_out[...] = g
    state[...] = leaving


def backward_kernel(
    proj, halo, entering, dg, par_x, par_bc, par_dt, dproj, gx, gbc, gdt, dstate, dhalo
):
    inner = par_x.shape[1]
    step = pl.program_id(0)
    last = pl.num_programs(0) - 1

    @pl.when(step == 0)
    def _():
        dstate[...] = jnp.zeros_like(dstate)
        dhalo[...] = jnp.zeros_like(dhalo)
        gx[...] = jnp.zeros_like(gx)
        gbc[...] = jnp.zeros_like(gbc)
        gdt[...] = jnp.zeros_like(gdt)

    live = jnp.where(step < last, 1.0, 0.0).astype(F32)
    head, tail = block_args(proj, halo, live, par_x, par_bc, par_dt, inner)
    _, pull = jax.vjp(block_mixer, *head, entering[0], *tail)
    (dz, dx, db, dc, ddt, dhx, dhb, dhc, dst, dxt, dbt, dct, dxb, dbb, dcb, dtb, dal, dsk) = pull(
        (dg[...], dstate[...])
    )
    dstate[...] = dst

    def joined(values, low, high):
        end = values.shape[0] - 8
        return jnp.concatenate([values[:end], values[end:] + dhalo[:, low:high]], axis=0).astype(
            BF16
        )

    at = 2 * inner
    dproj[:, :inner] = dz.astype(BF16)
    dproj[:, inner:at] = joined(dx, 0, inner)
    dproj[:, at : at + 128] = joined(db, inner, inner + 128)
    dproj[:, at + 128 : at + 256] = joined(dc, inner + 128, inner + 256)
    dproj[:, at + 256 : at + 256 + DTW] = ddt.astype(BF16)
    dhalo[:, :inner] = dhx
    dhalo[:, inner : inner + 128] = dhb
    dhalo[:, inner + 128 :] = dhc
    for k in range(4):
        gx[k : k + 1, :] += dxt[k]
        gbc[k : k + 1, :128] += dbt[k]
        gbc[k : k + 1, 128:] += dct[k]
    gx[4:5, :] += dxb
    gbc[4:5, :128] += dbb
    gbc[4:5, 128:] += dcb
    gx[5:6, :] += dsk
    gdt[0:1, :] += dtb
    gdt[1:2, :] += dal


def whole(shape):
    return pl.BlockSpec(shape, lambda i: (0,) * len(shape))


def run_forward(proj, par_x, par_bc, par_dt):
    rows, width = proj.shape
    inner = par_x.shape[1]
    blocks = rows // BLOCK
    lead = BLOCK // 8
    return pl.pallas_call(
        forward_kernel,
        grid=(blocks,),
        in_specs=[
            pl.BlockSpec((BLOCK, width), lambda i: (i, 0)),
            pl.BlockSpec((8, width), lambda i: (jnp.maximum(i * lead - 1, 0), 0)),
            whole(par_x.shape),
            whole(par_bc.shape),
            whole(par_dt.shape),
        ],
        out_specs=[
            pl.BlockSpec((BLOCK, inner), lambda i: (i, 0)),
            pl.BlockSpec((1, 128, inner), lambda i: (i, 0, 0)),
        ],
        out_shape=[
            jax.ShapeDtypeStruct((rows, inner), F32),
            jax.ShapeDtypeStruct((blocks, 128, inner), F32),
        ],
        scratch_shapes=[pltpu.VMEM((128, inner), F32)],
        compiler_params=pltpu.CompilerParams(vmem_limit_bytes=VMEM_BYTES),
        cost_estimate=pl.CostEstimate(
            flops=rows * inner * 20000, bytes_accessed=rows * width * 8, transcendentals=rows * 1024
        ),
    )(proj, proj, par_x, par_bc, par_dt)


def run_backward(proj, entering, dg, par_x, par_bc, par_dt):
    rows, width = proj.shape
    inner = par_x.shape[1]
    blocks = rows // BLOCK
    lead = BLOCK // 8
    top = blocks - 1
    return pl.pallas_call(
        backward_kernel,
        grid=(blocks,),
        in_specs=[
            pl.BlockSpec((BLOCK, width), lambda i: (top - i, 0)),
            pl.BlockSpec((8, width), lambda i: (jnp.maximum((top - i) * lead - 1, 0), 0)),
            pl.BlockSpec((1, 128, inner), lambda i: (top - i, 0, 0)),
            pl.BlockSpec((BLOCK, inner), lambda i: (top - i, 0)),
            whole(par_x.shape),
            whole(par_bc.shape),
            whole(par_dt.shape),
        ],
        out_specs=[
            pl.BlockSpec((BLOCK, width), lambda i: (top - i, 0)),
            whole(par_x.shape),
            whole(par_bc.shape),
            whole(par_dt.shape),
        ],
        out_shape=[
            jax.ShapeDtypeStruct((rows, width), BF16),
            jax.ShapeDtypeStruct(par_x.shape, F32),
            jax.ShapeDtypeStruct(par_bc.shape, F32),
            jax.ShapeDtypeStruct(par_dt.shape, F32),
        ],
        scratch_shapes=[pltpu.VMEM((128, inner), F32), pltpu.VMEM((8, inner + 256), F32)],
        compiler_params=pltpu.CompilerParams(vmem_limit_bytes=VMEM_BYTES),
        cost_estimate=pl.CostEstimate(
            flops=rows * inner * 60000, bytes_accessed=rows * width * 8, transcendentals=rows * 1024
        ),
    )(proj, proj, entering, dg, par_x, par_bc, par_dt)


def rows8(*members):
    stacked = jnp.concatenate([m.astype(F32) for m in members], axis=0)
    return jnp.pad(stacked, ((0, 8 - stacked.shape[0]), (0, 0)))


def body(
    inputs,
    cotangent,
    norm_gain,
    w_zx,
    w_bc,
    w_dt,
    dt_bias,
    a_log,
    d_skip,
    conv_x_w,
    conv_x_b,
    conv_bc_w,
    conv_bc_b,
    gate_gain,
    w_out,
):
    section_count = lax.axis_size("section")
    here = lax.axis_index("section")
    tensor_count = lax.axis_size("tensor")
    tensor_id = lax.axis_index("tensor")
    dp_count = lax.axis_size("dp")
    seq_dev, rows_own, width = inputs.shape
    length = rows_own * tensor_count
    inner = w_zx.shape[3]
    heads = w_dt.shape[2]
    mine = seq_dev // section_count
    total_inner = inner * tensor_count
    first = here == 0
    swap = [(0, 1), (1, 0)]

    def other(value):
        return lax.ppermute(value, "section", swap)

    def both(own):
        got = other(own)
        return jnp.where(first, own, got), jnp.where(first, got, own)

    w_all_own = jnp.concatenate(
        [
            w_zx[0].reshape(width, 2 * inner),
            w_bc[0],
            jnp.pad(w_dt[0], ((0, 0), (0, DTW - heads))),
        ],
        axis=1,
    )
    small_own = jnp.concatenate(
        [
            rows8(conv_x_w[0], conv_x_b, jnp.repeat(d_skip, HEAD, axis=1), gate_gain),
            rows8(conv_bc_w[0], conv_bc_b),
            rows8(*[jnp.pad(m, ((0, 0), (0, DTW - heads))) for m in (dt_bias, a_log)]),
            rows8(norm_gain),
        ],
        axis=1,
    )
    smalls = both(small_own)
    w_alls = both(w_all_own)
    w_outs = both(w_out[0])
    par = []
    for small in smalls:
        at = inner + 256
        par.append(
            dict(
                x=small[:, :inner],
                bc=small[:, inner:at],
                dt=small[:, at : at + DTW],
                gain=small[0:1, at + DTW :],
                gate=small[6:7, :inner],
            )
        )

    rows_in = lax.dynamic_slice_in_dim(inputs, here * mine, mine, 0)
    seeds = lax.dynamic_slice_in_dim(cotangent, here * mine, mine, 0)

    hidden_low = [rows_in[s] for s in range(mine)]
    kept = []
    outs = []
    for layer in range(2):
        p = par[layer]
        layer_kept = []
        layer_out = []
        for s in range(mine):
            hidden = hidden_low[s].astype(F32)
            scale_in = lax.rsqrt(jnp.mean(hidden * hidden, axis=-1, keepdims=True) + EPSILON)
            normed_own = (hidden * scale_in * p["gain"]).astype(BF16)
            normed = lax.all_gather(normed_own, "tensor", axis=0, tiled=True)
            proj = jnp.dot(normed, w_alls[layer], preferred_element_type=F32)
            gated, entering = run_forward(proj, p["x"], p["bc"], p["dt"])
            squares = lax.psum(jnp.sum(gated * gated, axis=-1), "tensor")
            partial = jnp.dot(
                (gated * p["gate"]).astype(BF16), w_outs[layer], preferred_element_type=F32
            ).astype(BF16)
            raw = lax.psum_scatter(partial, "tensor", scatter_dimension=0, tiled=True).astype(F32)
            scale_gate = lax.rsqrt(squares / total_inner + EPSILON)
            scale_own = lax.dynamic_slice_in_dim(scale_gate, tensor_id * rows_own, rows_own, 0)
            out_low = (hidden + scale_own[:, None] * raw).astype(BF16)
            layer_out.append(out_low)
            layer_kept.append((hidden, scale_in, normed, proj, gated, entering, raw, scale_gate))
        hidden_low = layer_out
        kept.append(layer_kept)
        outs.append(jnp.stack(layer_out))

    grad_low = [seeds[s] for s in range(mine)]
    grads = [None, None]
    grad_rows = [None, None]
    for layer in (1, 0):
        p = par[layer]
        layer_grad = []
        total = None
        for s in range(mine):
            hidden, scale_in, normed, proj, gated, entering, raw, scale_gate = kept[layer][s]
            own = grad_low[s].astype(F32)
            dot = lax.all_gather(jnp.sum(own * raw, axis=-1), "tensor", axis=0, tiled=True)
            full = lax.all_gather(grad_low[s], "tensor", axis=0, tiled=True)
            q = scale_gate[:, None]
            d_mixed = plain_dot(full, w_outs[layer], "nt", False)
            mixed = (gated * q * p["gate"]).astype(BF16)
            g_gate = jnp.sum(d_mixed * gated * q, axis=0)
            d_gated = q * p["gate"] * d_mixed - gated * (
                q * q * q * (dot[:, None] / total_inner)
            )
            d_proj, g_x, g_bc, g_dt = run_backward(
                proj, entering, d_gated, p["x"], p["bc"], p["dt"]
            )
            d_normed = plain_dot(d_proj, w_alls[layer], "nt", False).astype(BF16)
            d_in = lax.psum_scatter(
                d_normed, "tensor", scatter_dimension=0, tiled=True
            ).astype(F32)
            g_gain = jnp.sum(d_in * hidden * scale_in, axis=0)
            inner_dot = jnp.sum(hidden * p["gain"] * d_in, axis=-1, keepdims=True)
            d_hidden = (
                own
                + scale_in * p["gain"] * d_in
                - hidden * (scale_in * scale_in * scale_in * (inner_dot / width))
            )
            layer_grad.append(d_hidden)
            g_all = plain_dot(normed, d_proj, "tn", False)
            g_out = plain_dot(mixed, full, "tn", False)
            members = (g_all, g_out, g_x, g_bc, g_dt, g_gate, g_gain)
            total = members if total is None else tuple(a + b for a, b in zip(total, members))
        grad_rows[layer] = jnp.stack(layer_grad)
        grad_low = [g.astype(BF16) for g in layer_grad]
        grads[layer] = total

    def settle(pair, dtype):
        keep = jnp.where(first, pair[0], pair[1])
        send = jnp.where(first, pair[1], pair[0]).astype(dtype)
        return keep + other(send).astype(F32)

    def over_dp(value, dtype):
        low = value.astype(dtype)
        if dp_count == 2:
            return low.astype(F32) + lax.ppermute(low, "dp", swap).astype(F32)
        return lax.psum(low, "dp").astype(F32)

    g_all = settle([grads[0][0], grads[1][0]], BF16)
    g_out = settle([grads[0][1], grads[1][1]], BF16)

    def small_pack(g):
        x = jnp.concatenate([g[2][:6], g[5][None], jnp.zeros((1, inner), F32)], axis=0)
        shared = jnp.concatenate([g[3], jnp.broadcast_to(g[6][None] * 0.125, (8, width))], axis=1)
        return jnp.concatenate([x, g[4], shared], axis=1)

    small = settle([small_pack(grads[0]), small_pack(grads[1])], F32)
    at = inner + DTW
    shared_small, g_bc = lax.psum(
        (small[:, at:], g_all[:, 2 * inner : 2 * inner + 256]), ("tensor", "dp")
    )
    sharded = over_dp(small[:, :at], F32)
    g_zx = over_dp(g_all[:, : 2 * inner], BF16)
    g_dt = over_dp(g_all[:, 2 * inner + 256 :], BF16)[:, :heads]
    g_out = over_dp(g_out, BF16)

    def exchanged(pair):
        keep = jnp.where(first, pair[0], pair[1])
        got = other(jnp.where(first, pair[1], pair[0]))
        return jnp.concatenate(
            [jnp.where(first, keep, got), jnp.where(first, got, keep)], axis=0
        )[None]

    return (
        exchanged(outs),
        exchanged(grad_rows),
        jnp.sum(shared_small[:, 256:], axis=0)[None],
        g_zx.reshape(1, width, 2, inner),
        g_bc[None],
        g_dt[None],
        sharded[0:1, inner : inner + heads],
        sharded[1:2, inner : inner + heads],
        jnp.sum(sharded[5, :inner].reshape(heads, HEAD), axis=1)[None],
        sharded[None, 0:4, :inner],
        sharded[4:5, :inner],
        shared_small[None, 0:4, :256],
        shared_small[4:5, :256],
        sharded[6:7, :inner],
        g_out[None],
    )


def solution(mesh):
    specs_in = (
        P("dp", "tensor", None),
        P("dp", "tensor", None),
        P("section", None),
        P("section", None, None, "tensor"),
        P("section", None, None),
        P("section", None, "tensor"),
        P("section", "tensor"),
        P("section", "tensor"),
        P("section", "tensor"),
        P("section", None, "tensor"),
        P("section", "tensor"),
        P("section", None, None),
        P("section", None),
        P("section", "tensor"),
        P("section", "tensor", None),
    )
    specs_out = (
        P("section", "dp", "tensor", None),
        P("section", "dp", "tensor", None),
        *specs_in[2:],
    )
    return jax.shard_map(
        body, mesh=mesh, in_specs=specs_in, out_specs=specs_out, check_vma=False
    )
```

time: 2400 us -> 1240 us (0.52)
  other arithmetic: 433 us -> 40 us
  matrix products: 456 us -> 76 us
  local copies, waits for them, and re-layouts: 346 us -> 25.6 us
  waiting for transfers between devices: 951 us -> 775 us
  Pallas kernels: 0 us -> 106 us
    dot_general x87 -> x24, matrix products: 440 us -> 76 us  [the longest x16 49.9 us: plain_dot(): lax.dot_general(a.astype(BF16), b.astype(BF16), (DIMS[mode], ((), ())), p...]
    another operation x35 -> x2, other arithmetic: 187 us -> 4.13 us
    reduce_scatter x6 -> x8, waiting for transfers between devices: 612 us -> 454 us  [the longest x4 246 us: body(): lax.psum_scatter(d_normed, 'tensor', scatter_dimension=0, tiled=True)]
    reshape x26 -> x0, local copies, waits for them, and re-layouts: 110 us -> none  [the longest x15 68.5 us: state_scan(): return (within + carried).reshape(seq_count, length, head_count, head_size)]
    pallas_call x0 -> x8, Pallas kernels: none -> 106 us  [the longest x4 71.5 us: run_backward(): pl.pallas_call(backward_kernel, grid=(blocks,), in_specs=[pl.BlockSpec((B...]
    reduce_sum x44 -> x12, other arithmetic: 90.6 us -> 14.5 us  [the longest x2 5.49 us: body(): jnp.sum(own * raw, axis=-1)]
    all_gather x0 -> x4, blocking collectives: none -> 71.5 us  [body(): lax.all_gather(jnp.sum(own * raw, axis=-1), 'tensor', axis=0, tiled=True)]
    psum x2 -> x1, waiting for transfers between devices: 115 us -> 43.8 us  [body(): lax.psum((small[:, at:], g_all[:, 2 * inner:2 * inner + 256]), ('tensor',...]
  transfers between devices with their start and end apart: 18 -> 29, of which waited for: 15 -> 22; matrix products, arithmetic and copies ran while one was open for 19% -> 8% of each run, Pallas kernels for 0% -> 7%
where the time goes in v1:
time: 1240 us; the launch traced here: 1230 us
  waiting for transfers between devices  775 us (62%)
  blocking collectives  184 us (15%)
  Pallas kernels  106 us (9%)
  matrix products  76 us (6%)
  other arithmetic  40 us (3%)
  local copies, waits for them, and re-layouts  25.6 us (2%)
  between operations  15.2 us (1%)
    reduce_scatter x4, waiting for transfers between devices, body(): lax.psum_scatter(d_normed, 'tensor', scatter_dimension=0, tiled=True)  246 us
    reduce_scatter x4, waiting for transfers between devices, body(): lax.psum_scatter(partial, 'tensor', scatter_dimension=0, tiled=True)  208 us
    all_gather x4, waiting for transfers between devices, body(): normed = lax.all_gather(normed_own, 'tensor', axis=0, tiled=True)  159 us
    psum x1, blocking collectives, body(): lax.psum((small[:, at:], g_all[:, 2 * inner:2 * inner + 256]), ('tensor',...  73.7 us
    all_gather x4, blocking collectives, body(): lax.all_gather(jnp.sum(own * raw, axis=-1), 'tensor', axis=0, tiled=True)  71.5 us
    pallas_call x4, Pallas kernels, run_backward(): pl.pallas_call(backward_kernel, grid=(blocks,), in_specs=[pl.BlockSpec((B...  71.5 us
    all_gather x4, waiting for transfers between devices, body(): full = lax.all_gather(grad_low[s], 'tensor', axis=0, tiled=True)  69.8 us
    dot_general x16, matrix products, plain_dot(): lax.dot_general(a.astype(BF16), b.astype(BF16), (DIMS[mode], ((), ())), p...  49.9 us
  transfers between devices with their start and end apart: 29, of which 22 were waited for; matrix products, arithmetic and copies ran while one was open for 8% of the time, Pallas kernels for 7%

profile of v1, /device:TPU:0, one launch (start us, length us, event | category | flops | bytes accessed | tf_op | source)
XLA Modules:
  0.0 1230.3 jit_solution(17152561954073093633)
XLA Ops:
  19.6 3.8 collective-permute-done.2
  24.2 2.9 broadcast_select_fusion
  27.1 41.4 %all-gather.17.cloned.1.call-done = bf16[1024,1024]{1,0:T(8,128)(2,1)} async-done(((bf16[128,1024]{1,0:T(8,128)(2,1)}), bf16[1024,1024]{1,0:T(8,128)(2,1)}) %all-gather.17.cloned.1.call-update) | async-done | bytes 2097168 | tf_op jit(solution)/shard_map/all_gather | solution.py:384
  68.5 4.5 fusion.104.proj.halo
  73.0 8.5 shard_map.266
  81.6 2.0 convolution_convert_fusion.6
  83.7 35.3 %all-gather.15.cloned.1.call-done = bf16[1024,1024]{1,0:T(8,128)(2,1)} async-done(((bf16[128,1024]{1,0:T(8,128)(2,1)}), bf16[1024,1024]{1,0:T(8,128)(2,1)}) %all-gather.15.cloned.1.call-update) | async-done | bytes 2097168 | tf_op jit(solution)/shard_map/all_gather | solution.py:384
  119.0 4.5 fusion.103.proj.halo
  123.5 8.5 shard_map.265
  132.9 2.0 convolution_convert_fusion.7
  135.9 19.7 %all-reduce.8 = (f32[1024]{0:T(1024)S(1)}, f32[1024]{0:T(1024)S(1)}) all-reduce(f32[1024]{0:T(1024)S(1)} %multiply_reduce_fusion.6, f32[1024]{0:T(1024)S(1)} %multiply_reduce_fusion.7), channel_id=1, replica_groups=mesh['section'=2,'tensor'=8,'dp'=2] {'tensor'}, use_global_device_ids=true, to_apply=%region_6.7 | all-reduce | flops 2048 | bytes 16384 | tf_op jit(solution)/shard_map/psum | solution.py:387
  155.8 33.8 %reduce-scatter.11.cloned.1.call-done = bf16[128,1024]{1,0:T(8,128)(2,1)} async-done(((bf16[1024,1024]{1,0:T(8,128)(2,1)}), bf16[128,1024]{1,0:T(8,128)(2,1)}) %reduce-scatter.11.cloned.1.call-update) | async-done | bytes 262160 | tf_op jit(solution)/shard_map/reduce_scatter | solution.py:391
  189.6 70.7 %reduce-scatter.9.cloned.1.call-done = bf16[128,1024]{1,0:T(8,128)(2,1)} async-done(((bf16[1024,1024]{1,0:T(8,128)(2,1)}), bf16[128,1024]{1,0:T(8,128)(2,1)}) %reduce-scatter.9.cloned.1.call-update) | async-done | bytes 262160 | tf_op jit(solution)/shard_map/reduce_scatter | solution.py:391
  263.6 47.8 %all-gather.21.cloned.1.call-done = bf16[1024,1024]{1,0:T(8,128)(2,1)} async-done(((bf16[128,1024]{1,0:T(8,128)(2,1)}), bf16[1024,1024]{1,0:T(8,128)(2,1)}) %all-gather.21.cloned.1.call-update) | async-done | bytes 2097168 | tf_op jit(solution)/shard_map/all_gather | solution.py:384
  311.3 4.5 fusion.106.proj.halo
  315.9 8.5 shard_map.268
  325.3 2.0 convolution_convert_fusion.4
  327.4 34.3 %all-gather.19.cloned.1.call-done = bf16[1024,1024]{1,0:T(8,128)(2,1)} async-done(((bf16[128,1024]{1,0:T(8,128)(2,1)}), bf16[1024,1024]{1,0:T(8,128)(2,1)}) %all-gather.19.cloned.1.call-update) | async-done | bytes 2097168 | tf_op jit(solution)/shard_map/all_gather | solution.py:384
  361.7 4.5 fusion.105.proj.halo
  366.2 8.5 shard_map.267
  376.5 2.0 convolution_convert_fusion.5
  380.3 19.4 %all-reduce.7 = (f32[1024]{0:T(1024)S(1)}, f32[1024]{0:T(1024)S(1)}) all-reduce(f32[1024]{0:T(1024)S(1)} %multiply_reduce_fusion.4, f32[1024]{0:T(1024)S(1)} %multiply_reduce_fusion.5), channel_id=1, replica_groups=mesh['section'=2,'tensor'=8,'dp'=2] {'tensor'}, use_global_device_ids=true, to_apply=%region_14.15 | all-reduce | flops 2048 | bytes 16384 | tf_op jit(solution)/shard_map/psum | solution.py:387
  399.8 32.3 %reduce-scatter.15.cloned.1.call-done = bf16[128,1024]{1,0:T(8,128)(2,1)} async-done(((bf16[1024,1024]{1,0:T(8,128)(2,1)}), bf16[128,1024]{1,0:T(8,128)(2,1)}) %reduce-scatter.15.cloned.1.call-update) | async-done | bytes 262160 | tf_op jit(solution)/shard_map/reduce_scatter | solution.py:391
  432.1 70.8 %reduce-scatter.13.cloned.1.call-done = bf16[128,1024]{1,0:T(8,128)(2,1)} async-done(((bf16[1024,1024]{1,0:T(8,128)(2,1)}), bf16[128,1024]{1,0:T(8,128)(2,1)}) %reduce-scatter.13.cloned.1.call-update) | async-done | bytes 262160 | tf_op jit(solution)/shard_map/reduce_scatter | solution.py:391
  502.9 2.2 fusion.21
  505.8 18.4 %all-gather.4 = f32[8,1,128]{2,1,0:T(1,128)S(1)} all-gather(f32[1,1,128]{2,1,0:T(1,128)S(1)} %bitcast.201), channel_id=1, replica_groups=mesh['section'=2,'tensor'=8,'dp'=2] {'tensor'}, dimensions={0}, use_global_device_ids=true | all-gather | bytes 4608 | tf_op jit(solution)/shard_map/all_gather | solution.py:411
  524.2 29.4 %all-gather.29.cloned.1.call-done = bf16[1,1024,1024]{2,1,0:T(8,128)(2,1)} async-done(((bf16[1,128,1024]{2,1,0:T(8,128)(2,1)}), bf16[1,1024,1024]{2,1,0:T(8,128)(2,1)}) %all-gather.29.cloned.1.call-update) | async-done | bytes 2097168 | tf_op jit(solution)/shard_map/all_gather | solution.py:412
  553.6 3.2 multiply_reduce_fusion
  556.8 17.8 %shard_map.271 = (bf16[1024,896]{1,0:T(8,128)(2,1)S(1)}, f32[8,256]{1,0:T(8,128)S(1)}, f32[8,256]{1,0:T(8,128)S(1)}, f32[8,128]{1,0:T(8,128)S(1)}) custom-call(f32[1024,896]{1,0:T(8,128)} %copy-done.8, f32[1024,896]{1,0:T(8,128)} %copy-done.8, f32[4,128,256]{2,1,0:T(8,128)S(1)} %copy-done.19, f32[1024,256]{1,0:T(8,128)S(1)} %get-tuple-element.132.dg, ...), custom_call_target="tpu_custom_call" | custom-call | flops 15728640000 | bytes 7340032 | tf_op jit(solution)/shard_map/pallas_call | solution.py:262
  575.8 3.7 convolution_convert_fusion.1
  579.5 18.4 %all-gather.2 = f32[8,1,128]{2,1,0:T(1,128)S(1)} all-gather(f32[1,1,128]{2,1,0:T(1,128)S(1)} %bitcast.200), channel_id=1, replica_groups=mesh['section'=2,'tensor'=8,'dp'=2] {'tensor'}, dimensions={0}, use_global_device_ids=true | all-gather | bytes 4608 | tf_op jit(solution)/shard_map/all_gather | solution.py:411
  597.9 5.5 all-gather.27.cloned.1.call-done
  603.4 3.5 multiply_reduce_fusion.1
  606.9 17.8 %shard_map.269 = (bf16[1024,896]{1,0:T(8,128)(2,1)S(1)}, f32[8,256]{1,0:T(8,128)S(1)}, f32[8,256]{1,0:T(8,128)S(1)}, f32[8,128]{1,0:T(8,128)S(1)}) custom-call(f32[1024,896]{1,0:T(8,128)} %copy-done.7, f32[1024,896]{1,0:T(8,128)} %copy-done.7, f32[4,128,256]{2,1,0:T(8,128)S(1)} %copy-done.17, f32[1024,256]{1,0:T(8,128)S(1)} %get-tuple-element.134.dg, ...), custom_call_target="tpu_custom_call" | custom-call | flops 15728640000 | bytes 7340032 | tf_op jit(solution)/shard_map/pallas_call | solution.py:262
  625.9 3.7 convolution_convert_fusion.3
  629.8 44.2 %reduce-scatter.21.cloned.1.call-done = bf16[128,1024]{1,0:T(8,128)(2,1)} async-done(((bf16[1024,1024]{1,0:T(8,128)(2,1)}), bf16[128,1024]{1,0:T(8,128)(2,1)}) %reduce-scatter.21.cloned.1.call-update) | async-done | bytes 262160 | tf_op jit(solution)/shard_map/reduce_scatter | solution.py:424
  674.0 70.9 %reduce-scatter.17.cloned.1.call-done = bf16[128,1024]{1,0:T(8,128)(2,1)} async-done(((bf16[1024,1024]{1,0:T(8,128)(2,1)}), bf16[128,1024]{1,0:T(8,128)(2,1)}) %reduce-scatter.17.cloned.1.call-update) | async-done | bytes 262160 | tf_op jit(solution)/shard_map/reduce_scatter | solution.py:424
  746.4 3.3 fusion.15
  750.3 6.1 fusion.108
  756.5 18.2 %all-gather.5 = f32[8,1,128]{2,1,0:T(1,128)S(1)} all-gather(f32[1,1,128]{2,1,0:T(1,128)S(1)} %bitcast.203), channel_id=1, replica_groups=mesh['section'=2,'tensor'=8,'dp'=2] {'tensor'}, dimensions={0}, use_global_device_ids=true | all-gather | bytes 4608 | tf_op jit(solution)/shard_map/all_gather | solution.py:411
  774.7 16.5 %all-gather.3 = f32[8,1,128]{2,1,0:T(1,128)S(1)} all-gather(f32[1,1,128]{2,1,0:T(1,128)S(1)} %bitcast.202), channel_id=1, replica_groups=mesh['section'=2,'tensor'=8,'dp'=2] {'tensor'}, dimensions={0}, use_global_device_ids=true | all-gather | bytes 4608 | tf_op jit(solution)/shard_map/all_gather | solution.py:411
  791.2 7.1 all-gather.25.cloned.1.call-done
  798.4 3.1 multiply_reduce_fusion.2
  801.5 17.7 %shard_map.272 = (bf16[1024,896]{1,0:T(8,128)(2,1)S(1)}, f32[8,256]{1,0:T(8,128)S(1)}, f32[8,256]{1,0:T(8,128)S(1)}, f32[8,128]{1,0:T(8,128)S(1)}) custom-call(f32[1024,896]{1,0:T(8,128)} %copy-done.5, f32[1024,896]{1,0:T(8,128)} %copy-done.5, f32[4,128,256]{2,1,0:T(8,128)S(1)} %copy-done.15, f32[1024,256]{1,0:T(8,128)S(1)} %get-tuple-element.128.dg, ...), custom_call_target="tpu_custom_call" | custom-call | flops 15728640000 | bytes 7340032 | tf_op jit(solution)/shard_map/pallas_call | solution.py:262
  820.4 27.8 %all-gather.23.cloned.1.call-done = bf16[1024,1024]{1,0:T(8,128)(2,1)} async-done(((bf16[128,1024]{1,0:T(8,128)(2,1)}), bf16[1024,1024]{1,0:T(8,128)(2,1)}) %all-gather.23.cloned.1.call-update) | async-done | bytes 2097168 | tf_op jit(solution)/shard_map/all_gather | solution.py:412
  848.2 3.1 multiply_reduce_fusion.3
  851.3 18.3 %shard_map.270 = (bf16[1024,896]{1,0:T(8,128)(2,1)S(1)}, f32[8,256]{1,0:T(8,128)S(1)}, f32[8,256]{1,0:T(8,128)S(1)}, f32[8,128]{1,0:T(8,128)S(1)}) custom-call(f32[1024,896]{1,0:T(8,128)} %copy-done.6, f32[1024,896]{1,0:T(8,128)} %copy-done.6, f32[4,128,256]{2,1,0:T(8,128)S(1)} %copy-done.13, f32[1024,256]{1,0:T(8,128)S(1)} %get-tuple-element.130.dg, ...), custom_call_target="tpu_custom_call" | custom-call | flops 15728640000 | bytes 7340032 | tf_op jit(solution)/shard_map/pallas_call | solution.py:262
  869.6 2.2 fusion.107
  871.9 2.3 convolution_add_fusion.1
  875.1 2.5 select_convert_fusion
  877.7 3.8 collective-permute-done.6
  881.5 2.7 fusion.94
  885.3 5.7 convolution_convert_fusion
  891.2 5.7 convolution_convert_fusion.2
  898.2 2.6 fusion.1
  912.6 10.5 collective-permute-done.11
  924.2 27.5 %collective-permute-done.8 = bf16[1024,128]{0,1:T(8,128)(2,1)S(1)} collective-permute-done((bf16[1024,128]{0,1:T(8,128)(2,1)S(1)}, bf16[1024,128]{0,1:T(8,128)(2,1)S(1)}, u32[]{:S(2)}, u32[]{:S(2)}) %collective-permute-start.8) | collective-permute-done | bytes 262176 | tf_op jit(solution)/shard_map/ppermute | solution.py:451
  952.4 43.8 %all-reduce.11.cloned.1.call-done = f32[1,1024,256]{1,2,0:T(8,128)} async-done(((f32[1,1024,256]{1,2,0:T(8,128)}), f32[1,1024,256]{1,2,0:T(8,128)}) %all-reduce.11.cloned.1.call-update) | async-done | bytes 1048592 | tf_op jit(solution)/shard_map/psum | solution.py:464
  996.2 2.5 copy.37
  998.7 3.0 convert_add_fusion.1
  1001.7 4.2 copy.36
  1006.0 60.4 %reduce-scatter.23.cloned.1.call-done = bf16[128,1024]{1,0:T(8,128)(2,1)} async-done(((bf16[1024,1024]{1,0:T(8,128)(2,1)}), bf16[128,1024]{1,0:T(8,128)(2,1)}) %reduce-scatter.23.cloned.1.call-update) | async-done | bytes 262160 | tf_op jit(solution)/shard_map/reduce_scatter | solution.py:424
  1066.4 70.9 %reduce-scatter.19.cloned.1.call-done = bf16[128,1024]{1,0:T(8,128)(2,1)} async-done(((bf16[1024,1024]{1,0:T(8,128)(2,1)}), bf16[128,1024]{1,0:T(8,128)(2,1)}) %reduce-scatter.19.cloned.1.call-update) | async-done | bytes 262160 | tf_op jit(solution)/shard_map/reduce_scatter | solution.py:424
  1142.7 73.7 %psum.46 = f32[8,1280]{1,0:T(8,128)S(1)} all-reduce(f32[8,1280]{1,0:T(8,128)S(1)} %slice.140), channel_id=1, replica_groups=mesh['section'=2,'tensor'=8,'dp'=2] {'tensor','dp'}, use_global_device_ids=true, to_apply=%region_36.37 | all-reduce | flops 10240 | bytes 81920 | tf_op jit(solution)/shard_map/psum | solution.py:464
  (287 shorter events, 59.0 us)
Async XLA Ops:
  7.2 9.6 copy-start.39
  7.2 61.3 %all-gather.17.cloned.1.call-start = ((), (), s32[]{:S(2)}) async-start(), calls=%async_computation.10 | async-start | bytes 2359296 | tf_op jit(solution)/shard_map/all_gather | solution.py:384
  12.3 2.3 collective-permute-start
  12.8 5.4 copy-start.41
  14.6 3.8 copy-start.42
  16.7 102.3 %all-gather.15.cloned.1.call-start = ((), (), s32[]{:S(2)}) async-start(), calls=%async_computation.8 | async-start | bytes 2359296 | tf_op jit(solution)/shard_map/all_gather | solution.py:384
  18.5 171.0 %reduce-scatter.11.cloned.1.call-start = ((), (), s32[]{:S(2)}) async-start(), calls=%async_computation.11 | async-start | bytes 2359296 | tf_op jit(solution)/shard_map/reduce_scatter | solution.py:391
  18.7 5.5 collective-permute-start.1
  19.5 3.8 collective-permute-start.2
  24.2 108.7 %copy-start.25 = (bf16[256,1024]{1,0:T(8,128)(2,1)}, bf16[256,1024]{1,0:T(8,128)(2,1)S(1)}, u32[]{:S(2)}) copy-start(bf16[256,1024]{1,0:T(8,128)(2,1)S(1)} %get-tuple-element.145) | copy-start | bytes 1572868
  73.0 8.5 copy-start.5
  83.7 176.6 %reduce-scatter.9.cloned.1.call-start = ((), (), s32[]{:S(2)}) async-start(), calls=%async_computation.9 | async-start | bytes 2359296 | tf_op jit(solution)/shard_map/reduce_scatter | solution.py:391
  123.5 8.5 copy-start.6
  135.0 176.4 %all-gather.21.cloned.1.call-start = ((), (), s32[]{:S(2)}) async-start(), calls=%async_computation.14 | async-start | bytes 2359296 | tf_op jit(solution)/shard_map/all_gather | solution.py:384
  261.8 54.0 %copy-start.21 = (bf16[128,1024]{1,0:T(8,128)(2,1)}, bf16[128,1024]{1,0:T(8,128)(2,1)S(1)}, u32[]{:S(2)}) copy-start(bf16[128,1024]{1,0:T(8,128)(2,1)S(1)} %get-tuple-element.120) | copy-start | bytes 786436
  261.8 54.0 %copy-start.62 = (f32[128]{0:T(128)}, f32[128]{0:T(128)S(1)}, u32[]{:S(2)}) copy-start(f32[128]{0:T(128)S(1)} %get-tuple-element.119) | copy-start | bytes 1540
  261.8 54.0 %copy-start.64 = (f32[128]{0:T(128)}, f32[128]{0:T(128)S(1)}, u32[]{:S(2)}) copy-start(f32[128]{0:T(128)S(1)} %get-tuple-element.143) | copy-start | bytes 1540
  261.8 54.0 %copy-start.50 = (f32[128]{0:T(128)}, f32[128]{0:T(128)S(1)}, u32[]{:S(2)}) copy-start(f32[128]{0:T(128)S(1)} %add_rsqrt_fusion.4) | copy-start | bytes 1540
  261.9 54.0 %copy-start.52 = (f32[128]{0:T(128)}, f32[128]{0:T(128)S(1)}, u32[]{:S(2)}) copy-start(f32[128]{0:T(128)S(1)} %add_rsqrt_fusion.5) | copy-start | bytes 1540
  262.9 98.8 %all-gather.19.cloned.1.call-start = ((), (), s32[]{:S(2)}) async-start(), calls=%async_computation.12 | async-start | bytes 2359296 | tf_op jit(solution)/shard_map/all_gather | solution.py:384
  263.5 168.6 %reduce-scatter.15.cloned.1.call-start = ((), (), s32[]{:S(2)}) async-start(), calls=%async_computation.15 | async-start | bytes 2359296 | tf_op jit(solution)/shard_map/reduce_scatter | solution.py:391
  315.9 8.6 copy-start.8
  315.9 9.4 copy-start.26
  327.3 175.6 %reduce-scatter.13.cloned.1.call-start = ((), (), s32[]{:S(2)}) async-start(), calls=%async_computation.13 | async-start | bytes 2359296 | tf_op jit(solution)/shard_map/reduce_scatter | solution.py:391
  366.2 8.5 copy-start.7
  366.2 10.3 copy-start.27
  378.6 175.0 %all-gather.29.cloned.1.call-start = ((), (), s32[]{:S(2)}) async-start(), calls=%async_computation.24 | async-start | bytes 2359296 | tf_op jit(solution)/shard_map/all_gather | solution.py:412
  505.1 98.3 %all-gather.27.cloned.1.call-start = ((), (), s32[]{:S(2)}) async-start(), calls=%async_computation.23 | async-start | bytes 2359296 | tf_op jit(solution)/shard_map/all_gather | solution.py:412
  505.7 168.3 %reduce-scatter.21.cloned.1.call-start = ((), (), s32[]{:S(2)}) async-start(), calls=%async_computation.19 | async-start | bytes 2359296 | tf_op jit(solution)/shard_map/reduce_scatter | solution.py:424
  556.8 19.1 %copy-start.37 = (bf16[1024,896]{0,1:T(8,128)(2,1)S(1)}, bf16[1024,896]{0,1:T(8,128)(2,1)}, u32[]{:S(2)}) copy-start(bf16[1024,896]{0,1:T(8,128)(2,1)} %get-tuple-element.123) | copy-start | bytes 5505028
  579.5 165.4 %reduce-scatter.17.cloned.1.call-start = ((), (), s32[]{:S(2)}) async-start(), calls=%async_computation.16 | async-start | bytes 2359296 | tf_op jit(solution)/shard_map/reduce_scatter | solution.py:424
  603.4 3.5 copy-start.17
  606.9 19.0 %copy-start.38 = (bf16[1024,896]{0,1:T(8,128)(2,1)S(1)}, bf16[1024,896]{0,1:T(8,128)(2,1)}, u32[]{:S(2)}) copy-start(bf16[1024,896]{0,1:T(8,128)(2,1)} %get-tuple-element.123) | copy-start | bytes 5505028
  629.6 115.3 %copy-start.51 = (f32[128]{0:T(128)S(1)}, f32[128]{0:T(128)}, u32[]{:S(2)}) copy-start(f32[128]{0:T(128)} %copy-done.50) | copy-start | bytes 1540
  629.6 115.3 %copy-start.53 = (f32[128]{0:T(128)S(1)}, f32[128]{0:T(128)}, u32[]{:S(2)}) copy-start(f32[128]{0:T(128)} %copy-done.52) | copy-start | bytes 1540
  629.6 116.8 %copy-start.65 = (f32[128]{0:T(128)S(1)}, f32[128]{0:T(128)}, u32[]{:S(2)}) copy-start(f32[128]{0:T(128)} %copy-done.64) | copy-start | bytes 1540
  629.6 116.8 %copy-start.63 = (f32[128]{0:T(128)S(1)}, f32[128]{0:T(128)}, u32[]{:S(2)}) copy-start(f32[128]{0:T(128)} %copy-done.62) | copy-start | bytes 1540
  629.6 168.8 %all-gather.25.cloned.1.call-start = ((), (), s32[]{:S(2)}) async-start(), calls=%async_computation.20 | async-start | bytes 2359296 | tf_op jit(solution)/shard_map/all_gather | solution.py:412
  749.7 98.5 %all-gather.23.cloned.1.call-start = ((), (), s32[]{:S(2)}) async-start(), calls=%async_computation.17 | async-start | bytes 2359296 | tf_op jit(solution)/shard_map/all_gather | solution.py:412
  750.3 245.9 %all-reduce.11.cloned.1.call-start = ((), (), s32[]{:S(2)}) async-start(), calls=%async_computation.22 | async-start | bytes 2097152 | tf_op jit(solution)/shard_map/psum | solution.py:464
  851.3 18.3 %copy-start.11 = (bf16[1024,896]{1,0:T(8,128)(2,1)S(1)}, bf16[1024,896]{1,0:T(8,128)(2,1)}, u32[]{:S(2)}) copy-start(bf16[1024,896]{1,0:T(8,128)(2,1)} %copy-done.10) | copy-start | bytes 5505028
  851.3 18.3 %copy-start.66 = (bf16[1024,1024]{1,0:T(8,128)(2,1)S(1)}, bf16[1024,1024]{1,0:T(8,128)(2,1)}, u32[]{:S(2)}) copy-start(bf16[1024,1024]{1,0:T(8,128)(2,1)} %all-gather.17.cloned.1.call-done) | copy-start | bytes 6291460
  877.6 3.9 collective-permute-start.6
  885.2 181.1 %reduce-scatter.23.cloned.1.call-start = ((), (), s32[]{:S(2)}) async-start(), calls=%async_computation.21 | async-start | bytes 2359296 | tf_op jit(solution)/shard_map/reduce_scatter | solution.py:424
  891.0 246.3 %reduce-scatter.19.cloned.1.call-start = ((), (), s32[]{:S(2)}) async-start(), calls=%async_computation.18 | async-start | bytes 2359296 | tf_op jit(solution)/shard_map/reduce_scatter | solution.py:424
  905.3 2.0 collective-permute-start.10
  905.5 3.6 copy-start.20
  905.6 4.2 collective-permute-start.3
  907.5 15.5 %collective-permute-start.11 = (bf16[256,1024]{1,0:T(8,128)(2,1)S(1)}, bf16[256,1024]{1,0:T(8,128)(2,1)S(1)}, u32[]{:S(2)}, u32[]{:S(2)}) collective-permute-start(bf16[256,1024]{1,0:T(8,128)(2,1)S(1)} %add_convert_fusion), channel_id=1, source_target_pairs={{0,1},{1,0},{2,3},{3,2},{4,5},{5,4},{6,7},{7,6},{8,9},{9,8},{10,11... | collective-permute-start | bytes 1572872 | tf_op jit(solution)/shard_map/ppermute | solution.py:451
  909.2 89.5 %collective-permute-start.7 = (bf16[1024,512]{0,1:T(8,128)(2,1)S(1)}, bf16[1024,512]{0,1:T(8,128)(2,1)}, u32[]{:S(2)}, u32[]{:S(2)}) collective-permute-start(bf16[1024,512]{0,1:T(8,128)(2,1)S(1)} %slice.142), channel_id=1, source_target_pairs={{0,1},{1,0},{2,3},{3,2},{4,5},{5,4},{6,7},{7,6},{8,9},{9,8},{10,11... | collective-permute-start | bytes 3145736 | tf_op jit(solution)/shard_map/ppermute | solution.py:451
  911.1 40.7 %collective-permute-start.8 = (bf16[1024,128]{0,1:T(8,128)(2,1)S(1)}, bf16[1024,128]{0,1:T(8,128)(2,1)S(1)}, u32[]{:S(2)}, u32[]{:S(2)}) collective-permute-start(bf16[1024,128]{0,1:T(8,128)(2,1)S(1)} %slice.144), channel_id=1, source_target_pairs={{0,1},{1,0},{2,3},{3,2},{4,5},{5,4},{6,7},{7,6},{8,9},{9,8},{10,11... | collective-permute-start | bytes 786440 | tf_op jit(solution)/shard_map/ppermute | solution.py:451
  1001.7 135.6 %copy-start.24 = (bf16[4,128,1024]{2,1,0:T(8,128)(2,1)S(1)}, bf16[4,128,1024]{2,1,0:T(8,128)(2,1)}, u32[]{:S(2)}) copy-start(bf16[4,128,1024]{2,1,0:T(8,128)(2,1)} %param.15) | copy-start | bytes 3145732
  1001.7 135.6 %copy-start.43 = (f32[1,1024]{1,0:T(1,128)S(1)}, f32[1,1024]{1,0:T(1,128)}, u32[]{:S(2)}) copy-start(f32[1,1024]{1,0:T(1,128)} %copy-done.42) | copy-start | bytes 12292
  1001.7 135.6 %copy-start.47 = (f32[128]{0:T(128)S(1)}, f32[128]{0:T(128)}, u32[]{:S(2)}) copy-start(f32[128]{0:T(128)} %copy-done.46) | copy-start | bytes 1540
  1001.7 135.6 %copy-start.49 = (f32[128]{0:T(128)S(1)}, f32[128]{0:T(128)}, u32[]{:S(2)}) copy-start(f32[128]{0:T(128)} %copy-done.48) | copy-start | bytes 1540
  1001.7 137.1 %copy-start.45 = (f32[256]{0:T(256)S(1)}, f32[256]{0:T(256)}, u32[]{:S(2)}) copy-start(f32[256]{0:T(256)} %add.248) | copy-start | bytes 3076
  1001.7 137.2 %copy-start.55 = (f32[128]{0:T(128)S(1)}, f32[128]{0:T(128)}, u32[]{:S(2)}) copy-start(f32[128]{0:T(128)} %copy-done.54) | copy-start | bytes 1540
  1001.7 137.2 %copy-start.57 = (f32[128]{0:T(128)S(1)}, f32[128]{0:T(128)}, u32[]{:S(2)}) copy-start(f32[128]{0:T(128)} %copy-done.56) | copy-start | bytes 1540
  1001.7 137.2 %copy-start.32 = (bf16[128,1024]{1,0:T(8,128)(2,1)S(1)}, bf16[128,1024]{1,0:T(8,128)(2,1)}, u32[]{:S(2)}) copy-start(bf16[128,1024]{1,0:T(8,128)(2,1)} %get-tuple-element.112) | copy-start | bytes 786436
  1006.0 134.4 %copy-start.29 = (f32[1,128,1024]{2,1,0:T(8,128)S(1)}, f32[1,128,1024]{2,1,0:T(8,128)}, u32[]{:S(2)}) copy-start(f32[1,128,1024]{2,1,0:T(8,128)} %get-tuple-element.147) | copy-start | bytes 1572868
  1006.0 134.4 %copy-start.30 = (f32[1,128,1024]{2,1,0:T(8,128)S(1)}, f32[1,128,1024]{2,1,0:T(8,128)}, u32[]{:S(2)}) copy-start(f32[1,128,1024]{2,1,0:T(8,128)} %get-tuple-element.162) | copy-start | bytes 1572868
  1138.8 2.3 collective-permute-start.5
  1140.6 80.0 %collective-permute-start.4 = (f32[2,128,1024]{2,1,0:T(8,128)S(1)}, f32[2,128,1024]{2,1,0:T(8,128)}, u32[]{:S(2)}, u32[]{:S(2)}) collective-permute-start(f32[2,128,1024]{2,1,0:T(8,128)S(1)} %fusion.13), channel_id=1, source_target_pairs={{0,16},{16,0},{1,17},{17,1},{2,18},{18,2},{3,19},{19,3},{4,20},{20... | collective-permute-start | bytes 3145736 | tf_op jit(solution)/shard_map/ppermute | solution.py:331
  1141.2 77.0 %collective-permute-start.9 = (f32[8,384]{1,0:T(8,128)S(1)}, f32[8,384]{1,0:T(8,128)S(1)}, u32[]{:S(2)}, u32[]{:S(2)}) collective-permute-start(f32[8,384]{1,0:T(8,128)S(1)} %slice.147), channel_id=1, source_target_pairs={{0,1},{1,0},{2,3},{3,2},{4,5},{5,4},{6,7},{7,6},{8,9},{9,8},{10,11... | collective-permute-start | bytes 36872 | tf_op jit(solution)/shard_map/ppermute | solution.py:451
  (33 other events, 57.1 us)
Sparse Core Ops, SparseCore 0:
  16.8 51.6 all-gather.16
  71.2 47.7 all-gather.14
  123.1 66.3 reduce-scatter.10
  193.5 66.6 reduce-scatter.8
  263.0 48.2 all-gather.20
  313.9 47.7 all-gather.18
  365.8 66.2 reduce-scatter.14
  436.2 66.6 reduce-scatter.12
  505.3 48.2 all-gather.28
  555.5 47.8 all-gather.26
  607.5 66.4 reduce-scatter.20
  678.0 66.8 reduce-scatter.16
  749.8 48.5 all-gather.24
  800.4 47.7 all-gather.22
  885.4 110.7 all-reduce.10
  999.6 66.7 reduce-scatter.22
  1070.3 66.9 reduce-scatter.18
